TPU v7x, 32 devices: a whole 2x2x4 slice. The times are simulated.
32 devices in a mesh: ctx: 16 (over z, y, x), cand: 2 (over core).
Axes of the slice: x: 2, y: 2, z: 4, core: 2. Of those that a mesh axis runs over, the one named last changes fastest.
Arguments:
- history: bfloat16 [2048, 1024], P('ctx', 'cand'), may hold values from -6 to 6
- head_weights: bfloat16 [1024, 4096], P(None, 'cand'), may hold values from -0.1875 to 0.1875
- merge_weights: bfloat16 [1024, 1024], P('cand'), may hold values from -0.1875 to 0.1875
- cand_table: bfloat16 [1024, 1024], P('cand'), may hold values from -6 to 6
- user_weights: bfloat16 [1024, 512], P('cand'), may hold values from -0.1875 to 0.1875
- item_weights: bfloat16 [1024, 512], replicated, may hold values from -0.1875 to 0.1875
- score_weights: float32 [512], replicated, may hold values from -0.4 to 0.4
- request_points: int32 [64], replicated, may hold values from 0 to 2047, as said below
- candidate_owner: int32 [64, 512], P('ctx'), may hold values from 0 to 1
- candidate_row: int32 [64, 512], P('ctx'), may hold values from 0 to 511
- relevance: int32 [64, 512], P('ctx'), may hold values from 0 to 3
Outputs:
- losses: float32 [64], P('ctx')
- history_grad: float32 [2048, 1024], P('ctx', 'cand')
- grad_heads: float32 [1024, 4096], P('ctx', 'cand')
- grad_merge: float32 [1024, 1024], P('cand', 'ctx')
Inputs may be any that keep to these rules, and one draw needn't show every extreme that they name: `request_points`: the last request is made at the last position of the history.
All inputs are finite; a program needn't handle non-finite values.
Results may differ from a plain program's by a relative error of at most 0.012.
The roundings to bfloat16 on the way count: a program that leaves them out, or rounds other values in their place, can miss the bound.
Values may be sent and summed in bfloat16 or wider, within the bound.
A program may use at most 64 MiB of HBM per device.

v0:
```python
import jax
import jax.numpy as jnp
from jax import lax
from jax.sharding import PartitionSpec as P

HEAD = 128


norm_eps = 1e-05


def silu_slope(argument):
    sigmoid_part = jax.nn.sigmoid(argument)
    return sigmoid_part * (1.0 + argument * (1.0 - sigmoid_part))


def layer_norm(argument):
    centred = argument - jnp.mean(argument, -1, keepdims=True)
    inverse = lax.rsqrt(jnp.mean(centred * centred, -1, keepdims=True) + norm_eps)
    return (centred * inverse, inverse)


def norm_back(gradient, normed, inverse):
    return inverse * (
        gradient
        - jnp.mean(gradient, -1, keepdims=True)
        - normed * jnp.mean(gradient * normed, -1, keepdims=True)
    )


def place_scores(queries, key_heads, query_place, key_start):
    scaling = queries.shape[-1] ** (-0.5)
    logits = (
        jnp.einsum("qhd,khd->hqk", queries, key_heads, preferred_element_type=jnp.float32) * scaling
    )
    key_place = key_start + jnp.arange(key_heads.shape[0], dtype=jnp.int32)
    allowed = (key_place[None, :] <= query_place[:, None])[None]
    divisor = (query_place + 1).astype(jnp.float32)[None, :, None]
    return (logits, allowed, divisor)


def tile_scores(queries, key_heads, query_start, key_start):
    query_place = query_start + jnp.arange(queries.shape[0], dtype=jnp.int32)
    return place_scores(queries, key_heads, query_place, key_start)


def per_device(
    history,
    head_weights,
    merge_weights,
    cand_table,
    user_weights,
    item_weights,
    score_weights,
    request_points,
    candidate_owner,
    candidate_row,
    relevance,
):
    row_count = history.shape[0]
    slice_width = history.shape[1]
    first_row = lax.axis_index("ctx") * row_count
    cand_index = lax.axis_index("cand")
    features = lax.all_gather(history, "cand", axis=1, tiled=True)
    x_wide = features.astype(jnp.float32)
    x_normed, x_inverse = layer_norm(x_wide)
    x_low = x_normed.astype(jnp.bfloat16)
    before = jnp.dot(x_low, head_weights, preferred_element_type=jnp.float32)
    project = jax.nn.silu(before).astype(jnp.bfloat16)
    head_count = merge_weights.shape[0] // HEAD
    sections = project.reshape(row_count, head_count, 4, HEAD)
    gate_part = sections[:, :, 0]
    values = sections[:, :, 1]
    queries = sections[:, :, 2]
    key_heads = sections[:, :, 3]
    zero_heads = jnp.zeros((row_count, head_count, HEAD), jnp.float32)
    last_row = first_row + row_count - 1
    scaling = HEAD ** (-0.5)
    all_keys, all_values = (
        lax.all_gather(key_heads, "ctx", axis=0, tiled=True),
        lax.all_gather(values, "ctx", axis=0, tiled=True),
    )

    def forward_compute(current):
        logits, allowed, divisor = tile_scores(queries, all_keys, first_row, 0)
        weight = jnp.where(allowed, jax.nn.silu(logits) / divisor, 0.0).astype(jnp.bfloat16)
        return jnp.einsum("hqk,khd->qhd", weight, all_values, preferred_element_type=jnp.float32)

    attended = lax.cond(0 <= last_row, forward_compute, lambda current: current, zero_heads)
    normed, inverse = layer_norm(attended)
    gated = (
        (normed * gate_part.astype(jnp.float32))
        .astype(jnp.bfloat16)
        .reshape(row_count, head_count * HEAD)
    )
    head_total = lax.psum_scatter(
        jnp.dot(gated, merge_weights, preferred_element_type=jnp.float32),
        "cand",
        scatter_dimension=1,
        tiled=True,
    )
    layer_out = (history.astype(jnp.float32) + head_total).astype(jnp.bfloat16)
    positions = first_row + jnp.arange(row_count, dtype=jnp.int32)
    matches = (request_points[:, None] == positions[None, :]).astype(jnp.bfloat16)
    own_rows = lax.psum_scatter(
        jnp.dot(matches, layer_out, preferred_element_type=jnp.float32),
        "ctx",
        scatter_dimension=0,
        tiled=True,
    )
    user_part = jnp.dot(
        own_rows.astype(jnp.bfloat16), user_weights, preferred_element_type=jnp.float32
    )
    user_proj = lax.psum(user_part, "cand")
    item_proj = jnp.dot(cand_table, item_weights, preferred_element_type=jnp.float32)
    owned = candidate_owner == cand_index
    pre_score = user_proj[:, None, :] + item_proj[candidate_row]
    score_part = jnp.where(owned, jnp.sum(jax.nn.silu(pre_score) * score_weights, -1), 0.0)
    scores = lax.psum(score_part, "cand")
    log_total = jnp.log(jnp.sum(jnp.exp(scores), -1, keepdims=True))
    target = (relevance + 1).astype(jnp.float32)
    target = target / jnp.sum(target, -1, keepdims=True)
    losses = log_total[:, 0] - jnp.sum(target * scores, -1)
    d_score = jnp.exp(scores - log_total) - target
    d_pre = jnp.where(
        owned[:, :, None], d_score[:, :, None] * score_weights * silu_slope(pre_score), 0.0
    )
    d_user = lax.psum(jnp.sum(d_pre, 1), "cand")
    d_picked = jnp.dot(d_user, user_weights.astype(jnp.float32).T, precision=lax.Precision.HIGHEST)
    all_grads = lax.all_gather(d_picked, "ctx", axis=0, tiled=True)
    matches_all = (request_points[:, None] == positions[None, :]).astype(jnp.float32)
    d_layer = lax.dot_general(
        matches_all, all_grads, (((0,), (0,)), ((), ())), precision=lax.Precision.HIGHEST
    )
    d_full = lax.all_gather(d_layer, "cand", axis=1, tiled=True)
    d_gated = jnp.dot(d_full, merge_weights.astype(jnp.float32).T, precision=lax.Precision.HIGHEST)
    d_gated = d_gated.reshape(row_count, head_count, HEAD)
    d_gate = d_gated * normed
    d_attended = norm_back(d_gated * gate_part.astype(jnp.float32), normed, inverse).astype(
        jnp.bfloat16
    )
    merge_term = lax.dot_general(
        gated.astype(jnp.float32), d_full, (((0,), (0,)), ((), ())), precision=lax.Precision.HIGHEST
    )
    grad_merge = lax.psum_scatter(merge_term, "ctx", scatter_dimension=1, tiled=True)

    def query_compute(current):
        logits, allowed, divisor = tile_scores(queries, all_keys, first_row, 0)
        slopes = jnp.einsum(
            "qhd,khd->hqk", d_attended, all_values, preferred_element_type=jnp.float32
        )
        d_logit = jnp.where(allowed, slopes * silu_slope(logits) / divisor, 0.0).astype(
            jnp.bfloat16
        )
        return (
            jnp.einsum("hqk,khd->qhd", d_logit, all_keys, preferred_element_type=jnp.float32)
            * scaling
        )

    d_query = lax.cond(0 <= last_row, query_compute, lambda current: current, zero_heads)
    begin = jnp.int32(0)
    piece_queries = lax.all_gather(queries, "ctx", axis=0, tiled=True)
    piece_grads = lax.all_gather(d_attended, "ctx", axis=0, tiled=True)
    piece_rows = piece_queries.shape[0]

    def key_compute(current):
        logits, allowed, divisor = tile_scores(piece_queries, key_heads, begin, first_row)
        weight = jnp.where(allowed, jax.nn.silu(logits) / divisor, 0.0).astype(jnp.bfloat16)
        slopes = jnp.einsum("qhd,khd->hqk", piece_grads, values, preferred_element_type=jnp.float32)
        d_logit = jnp.where(allowed, slopes * silu_slope(logits) / divisor, 0.0).astype(
            jnp.bfloat16
        )
        key_grad = (
            jnp.einsum("hqk,qhd->khd", d_logit, piece_queries, preferred_element_type=jnp.float32)
            * scaling
        )
        value_grad = jnp.einsum(
            "hqk,qhd->khd", weight, piece_grads, preferred_element_type=jnp.float32
        )
        return (key_grad, value_grad)

    d_key, d_value = lax.cond(
        begin + piece_rows - 1 >= first_row,
        key_compute,
        lambda current: current,
        (zero_heads, zero_heads),
    )
    d_project = jnp.stack([d_gate, d_value, d_query, d_key], 2).reshape(
        row_count, head_count * 4 * HEAD
    )
    d_before = (d_project * silu_slope(before)).astype(jnp.bfloat16)
    grad_heads = lax.psum_scatter(
        lax.dot_general(
            x_low, d_before, (((0,), (0,)), ((), ())), preferred_element_type=jnp.float32
        ),
        "ctx",
        scatter_dimension=0,
        tiled=True,
    )
    normed_part = jnp.dot(d_before, head_weights.T, preferred_element_type=jnp.float32)
    column_start = cand_index * slice_width
    d_normed = lax.psum(normed_part, "cand")
    d_input = lax.dynamic_slice_in_dim(
        norm_back(d_normed, x_normed, x_inverse), column_start, slice_width, 1
    )
    history_grad = d_layer + d_input
    return (losses, history_grad, grad_heads, grad_merge)


def solution(mesh):
    return jax.shard_map(
        per_device,
        mesh=mesh,
        in_specs=(
            P("ctx", "cand"),
            P(None, "cand"),
            P("cand", None),
            P("cand", None),
            P("cand", None),
            P(),
            P(),
            P(),
            P("ctx", None),
            P("ctx", None),
            P("ctx", None),
        ),
        out_specs=(P("ctx"), P("ctx", "cand"), P("ctx", "cand"), P("cand", "ctx")),
        check_vma=False,
    )
```

profile of v0, /device:TPU:0, one launch (start us, length us, event | category | flops | bytes accessed | tf_op | source)
XLA Modules:
  0.0 678.0 jit_solution(8845420729739387904)
XLA Ops:
  7.2 2.5 all_gather.21
  10.1 4.1 multiply_convert_fusion.1
  14.6 0.8 fusion.56
  18.4 61.8 %all-gather.13.cloned.1.call-done = bf16[2048,4,1,128]{3,1,2,0:T(4,128)(2,1)} async-done(((bf16[128,4,1,128]{3,1,2,0:T(4,128)(2,1)}), bf16[2048,4,1,128]{3,1,2,0:T(4,128)(2,1)}) %all-gather.13.cloned.1.call-update) | async-done | bytes 2097168 | tf_op jit(solution)/shard_map/all_gather | solution.py:81
  80.2 62.9 %all-gather.11.cloned.1.call-done = bf16[2048,4,1,128]{3,0,1,2:T(8,128)(2,1)} async-done(((bf16[128,4,1,128]{3,0,1,2:T(8,128)(2,1)}), bf16[2048,4,1,128]{3,0,1,2:T(8,128)(2,1)}) %all-gather.11.cloned.1.call-update) | async-done | bytes 2097168 | tf_op jit(solution)/shard_map/all_gather | solution.py:80
  143.1 4.9 conditional.3
  143.3 4.6 fusion.55
  148.1 1.1 fusion.59
  152.5 1.9 fusion.60
  154.5 8.9 %gather_fusion = f32[2048,512]{1,0:T(8,128)} fusion(f32[512,512]{1,0:T(8,128)S(1)} %fusion.60, s32[2048]{0:T(1024)S(1)} %broadcast_clamp_fusion), kind=kCustom, calls=%fused_computation | custom fusion | bytes 8396800 | tf_op jit(solution)/shard_map/gather | solution.py:117
  163.4 1.2 fusion.36
  164.6 76.2 %all-reduce.5 = bf16[64,512]{1,0:T(8,128)(2,1)S(1)} all-reduce(f32[64,512]{1,0:T(8,128)S(1)} %fusion.36), channel_id=6, replica_groups=mesh['ctx'=16,'cand'=2] {'ctx'}, use_global_device_ids=true, to_apply=%region_7.8.clone | all-reduce | flops 32768 | bytes 196608
  241.0 2.5 psum.28
  243.5 3.7 multiply_reduce_fusion
  247.2 0.8 broadcast_select_fusion
  247.9 2.5 psum.29
  250.4 0.9 exponential_reduce_fusion
  251.8 0.7 exponential_subtract_fusion
  252.5 3.5 select_reduce_fusion
  256.0 2.5 psum.30
  259.0 36.2 %all-gather.3 = f32[16,4,512]{2,1,0:T(4,128)S(1)} all-gather(f32[1,4,512]{2,1,0:T(4,128)S(1)} %convolution_bitcast_fusion), channel_id=1, replica_groups=mesh['ctx'=16,'cand'=2] {'ctx'}, dimensions={0}, use_global_device_ids=true | all-gather | bytes 139264 | tf_op jit(solution)/shard_map/all_gather | solution.py:130
  295.3 1.1 fusion.42
  296.3 2.2 all_gather.25
  298.5 1.0 fusion.61
  299.5 0.8 fusion.41
  300.3 0.7 multiply_convert_fusion.2
  301.3 1.0 copy.91
  302.3 1.0 copy.92
  303.3 10.8 %conditional.5 = (f32[128,4,1,128]{0,3,1,2:T(8,128)S(1)}) conditional(s32[]{:T(128)} %convert_element_type.85, () %tuple.42, (s32[]{:T(128)}, bf16[128,4,128]{0,2,1:T(8,128)(2,1)}, bf16[2048,4,128]{2,1,0:T(4,128)(2,1)}, bf16[128,4,128]{2,0,1:T(8,128)(2,1)}, bf16[2048,4,128]{2,0,1:T(8,128)(2,1)}) %tuple.102), branch_computations={%region_20.21_spmd, %region_21.22_spmd} | conditional | flops 818217344 | bytes 14157836 | solution.py:160
  303.5 4.4 fusion.21
  307.9 6.1 fusion.25
  314.1 48.1 %all-gather.9.cloned.1.call-done = bf16[2048,4,128]{0,2,1:T(8,128)(2,1)} async-done(((bf16[128,4,128]{0,2,1:T(8,128)(2,1)}), bf16[2048,4,128]{0,2,1:T(8,128)(2,1)}) %all-gather.9.cloned.1.call-update) | async-done | bytes 2097168 | tf_op jit(solution)/shard_map/all_gather | solution.py:163
  362.3 16.5 %conditional.4 = (f32[128,4,1,128]{0,3,1,2:T(8,128)S(1)}, f32[128,4,1,128]{0,3,1,2:T(8,128)S(1)}) conditional(s32[]{:T(128)} %convert_element_type.95, () %tuple.40, (s32[]{:T(128)}, bf16[2048,4,128]{0,2,1:T(8,128)(2,1)}, bf16[128,4,128]{2,1,0:T(4,128)(2,1)S(1)}, bf16[2048,4,128]{2,0,1:T(8,128)(2,1)}, bf16[128,4,128]{2,0,1:T(8,128)(2,1)S(1)}) %tuple.100), branch_computations={%region_18.19_spmd, %region_19.20_spmd} | conditional | flops 1095045248 | bytes 23618580 | solution.py:182
  362.3 4.3 fusion.58
  366.7 6.8 %fusion.12 = f32[128,4,1,128]{3,0,1,2:T(8,128)S(1)} fusion(bf16[2048,4,128]{2,0,1:T(8,128)(2,1)} %get-tuple-element.43, f32[4,2048,128]{2,1,0:T(8,128)} %fusion.58, bf16[2048,4,128]{0,2,1:T(8,128)(2,1)} %get-tuple-element.90, f32[2048]{0:T(1024)S(1)} %add_convert_fusion.1, pred[2048,128]{1,0:T(8,128)(4,1)S(1)} %iota_compare_fusion.1, ...), kind=kOutput, calls=%fused_computation.18 | convolution fusion | flops 549519360 | bytes 9052160 | tf_op jit(solution)/shard_map/cond/branch_1_fun/hqk,qhd->khd/dot_general | solution.py:174
  373.7 5.0 fusion.10
  379.5 1.2 pad_maximum_fusion
  380.7 1.4 copy.60
  382.2 2.6 reshape.166
  384.8 1.9 multiply_convert_fusion
  386.8 4.7 fusion.62
  391.6 2.4 fusion.63
  394.1 4.6 fusion.37
  398.7 9.9 %all-reduce.4.cloned.1.call-done = f32[128,1024]{1,0:T(8,128)} async-done(((f32[128,1024]{1,0:T(8,128)}), f32[128,1024]{1,0:T(8,128)}) %all-reduce.4.cloned.1.call-update) | async-done | bytes 524304 | tf_op jit(solution)/shard_map/psum | solution.py:202
  408.6 1.3 fusion.54
  409.9 1.8 fusion.35
  411.7 81.4 %reduce-scatter.8.cloned.1.call-done = f32[512,64]{0,1:T(8,128)} async-done(((f32[512,1024]{0,1:T(8,128)}), f32[512,64]{0,1:T(8,128)}) %reduce-scatter.8.cloned.1.call-update) | async-done | bytes 131088 | tf_op jit(solution)/shard_map/reduce_scatter | solution.py:145
  493.1 178.0 %reduce-scatter.6.cloned.1.call-done = f32[64,2048]{1,0:T(8,128)} async-done(((f32[1024,2048]{1,0:T(8,128)}), f32[64,2048]{1,0:T(8,128)}) %reduce-scatter.6.cloned.1.call-update) | async-done | bytes 524304 | tf_op jit(solution)/shard_map/reduce_scatter | solution.py:192
  (97 shorter events, 10.0 us)
Async XLA Ops:
  7.2 145.4 %copy-start = (bf16[512,1024]{1,0:T(8,128)(2,1)S(1)}, bf16[512,1024]{1,0:T(8,128)(2,1)}, u32[]{:S(2)}) copy-start(bf16[512,1024]{1,0:T(8,128)(2,1)} %param.20) | copy-start | bytes 3145732
  7.2 73.0 %all-gather.13.cloned.1.call-start = ((), (), s32[]{:S(2)}) async-start(), calls=%async_computation.9 | async-start | bytes 2228224 | tf_op jit(solution)/shard_map/all_gather | solution.py:81
  9.9 4.3 copy-start.17
  10.1 4.1 copy-start.15
  15.3 0.7 copy-start.3
  15.3 127.7 %copy-start.4 = (bf16[128,4,1,128]{3,2,1,0:T(2,128)(2,1)}, bf16[128,4,1,128]{3,2,1,0:T(2,128)(2,1)S(1)}, u32[]{:S(2)}) copy-start(bf16[128,4,1,128]{3,2,1,0:T(2,128)(2,1)S(1)} %get-tuple-element.119) | copy-start | bytes 393220
  16.7 126.3 %all-gather.11.cloned.1.call-start = ((), (), s32[]{:S(2)}) async-start(), calls=%async_computation.8 | async-start | bytes 2228224 | tf_op jit(solution)/shard_map/all_gather | solution.py:80
  17.5 145.9 %reduce-scatter.4.cloned.1.call-start = ((), (), s32[]{:S(2)}) async-start(), calls=%async_computation.3 | async-start | bytes 786432 | tf_op jit(solution)/shard_map/reduce_scatter | solution.py:96
  143.1 5.0 copy-start.1
  143.1 7.5 %copy-start.19 = (s32[4,512]{1,0:T(4,128)S(1)}, s32[4,512]{1,0:T(4,128)}, u32[]{:S(2)}) copy-start(s32[4,512]{1,0:T(4,128)} %param.26) | copy-start | bytes 24580
  143.1 7.5 %copy-start.14 = (s32[4,512]{1,0:T(4,128)S(1)}, s32[4,512]{1,0:T(4,128)}, u32[]{:S(2)}) copy-start(s32[4,512]{1,0:T(4,128)} %param.27) | copy-start | bytes 24580
  143.1 8.2 %copy-start.20 = (u32[32]{0:T(128)S(1)}, u32[32]{0:T(128)}, u32[]{:S(2)}) copy-start(u32[32]{0:T(128)} %constant.92) | copy-start | bytes 388
  148.1 4.4 copy-start.7
  149.3 164.9 %all-gather.15.cloned.1.call-start = ((), (), s32[]{:S(2)}) async-start(), calls=%async_computation.10 | async-start | bytes 2228224 | tf_op jit(solution)/shard_map/all_gather | solution.py:162
  150.0 212.2 %all-gather.9.cloned.1.call-start = ((), (), s32[]{:S(2)}) async-start(), calls=%async_computation.4 | async-start | bytes 2228224 | tf_op jit(solution)/shard_map/all_gather | solution.py:163
  154.5 8.9 %copy-start.13 = (bf16[128,512]{1,0:T(8,128)(2,1)S(1)}, bf16[128,512]{1,0:T(8,128)(2,1)}, u32[]{:S(2)}) copy-start(bf16[128,512]{1,0:T(8,128)(2,1)} %param.17) | copy-start | bytes 393220
  154.5 86.3 %copy-start.5 = (bf16[512,512]{1,0:T(8,128)(2,1)S(1)}, bf16[512,512]{1,0:T(8,128)(2,1)}, u32[]{:S(2)}) copy-start(bf16[512,512]{1,0:T(8,128)(2,1)} %param.21) | copy-start | bytes 1572868
  243.5 15.1 %copy-start.6 = (bf16[512,512]{1,0:T(8,128)(2,1)S(1)}, bf16[512,512]{1,0:T(8,128)(2,1)}, u32[]{:S(2)}) copy-start(bf16[512,512]{1,0:T(8,128)(2,1)} %param.21) | copy-start | bytes 1572868
  247.1 51.4 %copy-start.2 = (bf16[512,1024]{1,0:T(8,128)(2,1)S(1)}, bf16[512,1024]{1,0:T(8,128)(2,1)}, u32[]{:S(2)}) copy-start(bf16[512,1024]{1,0:T(8,128)(2,1)} %param.19) | copy-start | bytes 3145732
  301.1 107.5 %all-reduce.4.cloned.1.call-start = ((), (), s32[]{:S(2)}) async-start(), calls=%async_computation.5 | async-start | bytes 1048576 | tf_op jit(solution)/shard_map/psum | solution.py:202
  314.1 48.2 %copy-start.12 = (f32[128,4,1,128]{0,3,1,2:T(8,128)}, f32[128,4,1,128]{0,3,1,2:T(8,128)S(1)}, u32[]{:S(2)}) copy-start(f32[128,4,1,128]{0,3,1,2:T(8,128)S(1)} %get-tuple-element.101) | copy-start | bytes 786436
  362.3 17.3 %copy-start.9 = (f32[128,4,1,128]{0,3,1,2:T(8,128)S(1)}, f32[128,4,1,128]{0,3,1,2:T(8,128)}, u32[]{:S(2)}) copy-start(f32[128,4,1,128]{0,3,1,2:T(8,128)} %get-tuple-element.120) | copy-start | bytes 786436
  378.8 0.7 copy-start.10
  378.8 0.8 copy-start.11
  384.8 6.8 copy-start.8
  386.8 7.3 %copy-start.16 = (f32[128]{0:T(128)S(1)}, f32[128]{0:T(128)}, u32[]{:S(2)}) copy-start(f32[128]{0:T(128)} %copy-done.15) | copy-start | bytes 1540
  386.8 7.3 %copy-start.18 = (f32[128]{0:T(128)S(1)}, f32[128]{0:T(128)}, u32[]{:S(2)}) copy-start(f32[128]{0:T(128)} %copy-done.17) | copy-start | bytes 1540
  391.5 101.6 %reduce-scatter.8.cloned.1.call-start = ((), (), s32[]{:S(2)}) async-start(), calls=%async_computation.7 | async-start | bytes 2228224 | tf_op jit(solution)/shard_map/reduce_scatter | solution.py:145
  394.0 277.1 %reduce-scatter.6.cloned.1.call-start = ((), (), s32[]{:S(2)}) async-start(), calls=%async_computation.6 | async-start | bytes 8912896 | tf_op jit(solution)/shard_map/reduce_scatter | solution.py:192
Sparse Core Ops, SparseCore 0:
  16.9 63.2 all-gather.12
  83.5 59.5 all-gather.10
  149.4 6.7 reduce-scatter.3
  159.1 62.8 all-gather.14
  301.2 61.0 all-gather.8
  391.6 16.9 all-reduce.3
  411.4 81.6 reduce-scatter.7
  496.0 175.1 reduce-scatter.5
where the time goes:
time: 680 us; the launch traced here: 678 us
  waiting for transfers between devices  442 us (65%)
  blocking collectives  125 us (18%)
  matrix products  53.8 us (8%)
  local copies, waits for them, and re-layouts  21.5 us (3%)
  other arithmetic  20 us (3%)
  between operations  15.1 us (2%)
    reduce_scatter x1, waiting for transfers between devices, per_device(): lax.psum_scatter(lax.dot_general(x_low, d_before, (((0,), (0,)), ((), ())...  178 us
    reduce_scatter x1, waiting for transfers between devices, per_device(): lax.psum_scatter(merge_term, 'ctx', scatter_dimension=1, tiled=True)  81.4 us
    unnamed x1, blocking collectives  76.2 us
    all_gather x1, waiting for transfers between devices, per_device(): lax.all_gather(key_heads, 'ctx', axis=0, tiled=True)  62.9 us
    all_gather x1, waiting for transfers between devices, per_device(): lax.all_gather(values, 'ctx', axis=0, tiled=True)  61.8 us
    all_gather x1, waiting for transfers between devices, per_device(): piece_grads = lax.all_gather(d_attended, 'ctx', axis=0, tiled=True)  48.1 us
    all_gather x1, blocking collectives, per_device(): all_grads = lax.all_gather(d_picked, 'ctx', axis=0, tiled=True)  36.2 us
  transfers between devices with their start and end apart: 8, of which 6 were waited for; matrix products, arithmetic and copies ran while one was open for 8% of the time, Pallas kernels for 0%

commit v1 on v0

v1 whole, which is shorter than its diff:
```python
import jax
import jax.numpy as jnp
from jax import lax
from jax.sharding import PartitionSpec as P

HEAD = 128
norm_eps = 1e-05
HIGHEST = lax.Precision.HIGHEST
F32 = jnp.float32
BF16 = jnp.bfloat16


def silu_slope(argument):
    sigmoid_part = jax.nn.sigmoid(argument)
    return sigmoid_part * (1.0 + argument * (1.0 - sigmoid_part))


def layer_norm(argument):
    centred = argument - jnp.mean(argument, -1, keepdims=True)
    inverse = lax.rsqrt(jnp.mean(centred * centred, -1, keepdims=True) + norm_eps)
    return (centred * inverse, inverse)


def norm_back(gradient, normed, inverse):
    return inverse * (
        gradient
        - jnp.mean(gradient, -1, keepdims=True)
        - normed * jnp.mean(gradient * normed, -1, keepdims=True)
    )


def mm(left, right):
    return jnp.dot(left, right, preferred_element_type=F32)


def gather_history(history):
    rows = lax.all_gather(history, "ctx", axis=0, tiled=True)
    return lax.all_gather(rows, "cand", axis=1, tiled=True)


def gather_user_grad(part):
    return lax.all_gather(lax.psum(part, "cand"), "ctx", axis=0, tiled=True)


def per_device(
    history,
    head_weights,
    merge_weights,
    cand_table,
    user_weights,
    item_weights,
    score_weights,
    request_points,
    candidate_owner,
    candidate_row,
    relevance,
):
    row_count, slice_width = history.shape
    width = head_weights.shape[0]
    ctx_index = lax.axis_index("ctx")
    cand_index = lax.axis_index("cand")
    ctx_count = lax.axis_size("ctx")
    first_row = ctx_index * row_count
    heads = merge_weights.shape[0] // HEAD
    cols = heads * HEAD
    requests = request_points.shape[0]
    own_requests = candidate_row.shape[0]
    scaling = HEAD ** (-0.5)

    sections = head_weights.reshape(width, heads, 4, HEAD)
    gate_w, value_w, query_w, key_w = (
        sections[:, :, index].reshape(width, cols) for index in range(4)
    )
    item_proj = mm(cand_table, item_weights)
    user_full = lax.all_gather(user_weights, "cand", axis=0, tiled=True)

    features = gather_history(history)
    length = features.shape[0]
    x_low = layer_norm(features.astype(F32))[0].astype(BF16)

    picks = (request_points[:, None] == jnp.arange(length, dtype=jnp.int32)[None, :]).astype(BF16)
    x_requests = mm(picks, x_low).astype(BF16)
    raw_requests = mm(picks, features)

    before_key = mm(x_low, key_w)
    before_value = mm(x_low, value_w)
    before_query = mm(x_requests, query_w)
    before_gate = mm(x_requests, gate_w)

    def split(array):
        return array.reshape(array.shape[0], heads, HEAD)

    key_heads = split(jax.nn.silu(before_key).astype(BF16))
    values = split(jax.nn.silu(before_value).astype(BF16))
    queries = split(jax.nn.silu(before_query).astype(BF16))
    gate_part = split(jax.nn.silu(before_gate).astype(BF16)).astype(F32)

    logits = jnp.einsum("qhd,khd->hqk", queries, key_heads, preferred_element_type=F32) * scaling
    allowed = (jnp.arange(length, dtype=jnp.int32)[None, :] <= request_points[:, None])[None]
    divisor = (request_points + 1).astype(F32)[None, :, None]
    weight = jnp.where(allowed, jax.nn.silu(logits) / divisor, 0.0).astype(BF16)
    attended = jnp.einsum("hqk,khd->qhd", weight, values, preferred_element_type=F32)
    normed, inverse = layer_norm(attended)
    gated = (normed * gate_part).astype(BF16).reshape(requests, cols)

    def own(array):
        return lax.dynamic_slice_in_dim(array, ctx_index * own_requests, own_requests, 0)

    head_total = lax.psum(mm(own(gated), merge_weights), "cand")
    layer_out = (own(raw_requests) + head_total).astype(BF16)
    user_proj = mm(layer_out, user_full)

    owned = candidate_owner == cand_index
    table_rows = jnp.arange(cand_table.shape[0], dtype=jnp.int32)
    hits = owned[:, :, None] & (candidate_row[:, :, None] == table_rows)
    pre_score = user_proj[:, None, :] + item_proj[None]
    row_scores = jnp.sum(jax.nn.silu(pre_score) * score_weights, -1)
    scores = lax.psum(jnp.sum(jnp.where(hits, row_scores[:, None, :], 0.0), -1), "cand")
    log_total = jnp.log(jnp.sum(jnp.exp(scores), -1, keepdims=True))
    target = (relevance + 1).astype(F32)
    target = target / jnp.sum(target, -1, keepdims=True)
    losses = log_total[:, 0] - jnp.sum(target * scores, -1)
    d_score = jnp.exp(scores - log_total) - target
    row_grads = jnp.sum(jnp.where(hits, d_score[:, :, None], 0.0), 1)
    user_part = jnp.sum(row_grads[:, :, None] * silu_slope(pre_score), 1) * score_weights
    d_user = gather_user_grad(user_part)

    same = request_points[:, None] == request_points[None, :]
    order = jnp.arange(requests, dtype=jnp.int32)
    earlier = jnp.any(same & (order[None, :] < order[:, None]), 1)
    merge_same = (same & ~earlier[:, None]).astype(F32)
    d_user = jnp.dot(merge_same, d_user, precision=HIGHEST)
    d_picked = jnp.dot(d_user, user_full.astype(F32).T, precision=HIGHEST)
    d_gated = split(jnp.dot(d_picked, merge_weights.astype(F32).T, precision=HIGHEST))
    d_gate = (d_gated * normed).reshape(requests, cols)
    d_attended = norm_back(d_gated * gate_part, normed, inverse).astype(BF16)

    merge_cols = width // ctx_count
    own_picked = lax.dynamic_slice_in_dim(d_picked, ctx_index * merge_cols, merge_cols, 1)
    grad_merge = lax.dot_general(
        gated.astype(F32), own_picked, (((0,), (0,)), ((), ())), precision=HIGHEST
    )

    slopes = jnp.einsum("qhd,khd->hqk", d_attended, values, preferred_element_type=F32)
    d_logit = jnp.where(allowed, slopes * silu_slope(logits) / divisor, 0.0).astype(BF16)
    d_query = jnp.einsum("hqk,khd->qhd", d_logit, key_heads, preferred_element_type=F32) * scaling
    d_key = jnp.einsum("hqk,qhd->khd", d_logit, queries, preferred_element_type=F32) * scaling
    d_value = jnp.einsum("hqk,qhd->khd", weight, d_attended, preferred_element_type=F32)

    d_before_key = (d_key.reshape(length, cols) * silu_slope(before_key)).astype(BF16)
    d_before_value = (d_value.reshape(length, cols) * silu_slope(before_value)).astype(BF16)
    d_before_query = (d_query.reshape(requests, cols) * silu_slope(before_query)).astype(BF16)
    d_before_gate = (d_gate * silu_slope(before_gate)).astype(BF16)

    def own_features(array):
        return lax.dynamic_slice_in_dim(array, ctx_index * merge_cols, merge_cols, 1)

    def grad_of(rows, grads):
        return split(lax.dot_general(rows, grads, (((0,), (0,)), ((), ())), preferred_element_type=F32))

    x_own = own_features(x_low)
    x_own_requests = own_features(x_requests)
    grad_heads = jnp.stack(
        [
            grad_of(x_own_requests, d_before_gate),
            grad_of(x_own, d_before_value),
            grad_of(x_own_requests, d_before_query),
            grad_of(x_own, d_before_key),
        ],
        2,
    ).reshape(merge_cols, 4 * cols)

    def own_rows(array):
        return lax.dynamic_slice_in_dim(array, first_row, row_count, 0)

    positions = first_row + jnp.arange(row_count, dtype=jnp.int32)
    places = positions[:, None] == request_points[None, :]
    low_places = places.astype(BF16)
    transposed = (((1,), (1,)), ((), ()))

    def back(grads, weights):
        return lax.dot_general(grads, weights, transposed, preferred_element_type=F32)

    d_normed = lax.psum(
        back(own_rows(d_before_key), key_w)
        + back(own_rows(d_before_value), value_w)
        + back(mm(low_places, d_before_query).astype(BF16), query_w)
        + back(mm(low_places, d_before_gate).astype(BF16), gate_w),
        "cand",
    )
    x_normed, x_inverse = layer_norm(own_rows(features).astype(F32))
    column_start = cand_index * slice_width
    d_input = lax.dynamic_slice_in_dim(
        norm_back(d_normed, x_normed, x_inverse), column_start, slice_width, 1
    )
    picked_cols = lax.dynamic_slice_in_dim(d_picked, column_start, slice_width, 1)
    d_layer = jnp.dot(places.astype(F32), picked_cols, precision=HIGHEST)
    history_grad = d_layer + d_input
    return (losses, history_grad, grad_heads, grad_merge)


def solution(mesh):
    return jax.shard_map(
        per_device,
        mesh=mesh,
        in_specs=(
            P("ctx", "cand"),
            P(None, "cand"),
            P("cand", None),
            P("cand", None),
            P("cand", None),
            P(),
            P(),
            P(),
            P("ctx", None),
            P("ctx", None),
            P("ctx", None),
        ),
        out_specs=(P("ctx"), P("ctx", "cand"), P("ctx", "cand"), P("cand", "ctx")),
        check_vma=False,
    )
```

time: 680 us -> 262 us (0.39)
  waiting for transfers between devices: 442 us -> 80.2 us
  blocking collectives: 125 us -> 50.6 us
  other arithmetic: 20 us -> 38.4 us
    reduce_scatter x3 -> x0, waiting for transfers between devices: 259 us -> none  [the longest x1 178 us: per_device(): lax.psum_scatter(lax.dot_general(x_low, d_before, (((0,), (0,)), ((), ())...]
    all_gather x4 -> x3, waiting for transfers between devices: 173 us -> 66.3 us  [the longest x1 66.3 us: gather_history(): rows = lax.all_gather(history, 'ctx', axis=0, tiled=True)]
    unnamed x1 -> x0, blocking collectives: 76.2 us -> none
    gather x1 -> x0, local copies, waits for them, and re-layouts: 8.91 us -> none  [per_device(): pre_score = user_proj[:, None, :] + item_proj[candidate_row]]
    dot_general x16 -> x28, matrix products: 52.8 us -> 55 us  [the longest x9 20.3 us: mm(): return jnp.dot(left, right, preferred_element_type=F32)]
    all_gather x3 -> x1, blocking collectives: 40.9 us -> 40.8 us  [gather_user_grad(): return lax.all_gather(lax.psum(part, 'cand'), 'ctx', axis=0, tiled=True)]
  transfers between devices with their start and end apart: 8 -> 4, of which waited for: 6 -> 2; matrix products, arithmetic and copies ran while one was open for 8% -> 18% of each run, Pallas kernels for 0% -> 0%
where the time goes in v1:
time: 262 us; the launch traced here: 261 us
  waiting for transfers between devices  80.2 us (31%)
  matrix products  55 us (21%)
  blocking collectives  50.6 us (19%)
  other arithmetic  38.4 us (15%)
  local copies, waits for them, and re-layouts  22.3 us (9%)
  between operations  14.3 us (5%)
    all_gather x1, waiting for transfers between devices, gather_history(): rows = lax.all_gather(history, 'ctx', axis=0, tiled=True)  66.3 us
    all_gather x1, blocking collectives, gather_user_grad(): return lax.all_gather(lax.psum(part, 'cand'), 'ctx', axis=0, tiled=True)  40.8 us
    dot_general x9, matrix products, mm(): return jnp.dot(left, right, preferred_element_type=F32)  20.3 us
    psum x1, waiting for transfers between devices, per_device(): lax.psum(back(own_rows(d_before_key), key_w) + back(own_rows(d_before_val...  12.5 us
    unnamed x74, local copies, waits for them, and re-layouts  11.1 us
    dot_general x4, matrix products, grad_of(): lax.dot_general(rows, grads, (((0,), (0,)), ((), ())), preferred_element_...  7.43 us
    dot_general x4, matrix products, back(): lax.dot_general(grads, weights, transposed, preferred_element_type=F32)  6.94 us
    another operation x5, local copies, waits for them, and re-layouts, per_device(): jnp.stack([grad_of(x_own_requests, d_before_gate), grad_of(x_own, d_befor...  6.05 us
  transfers between devices with their start and end apart: 4, of which 2 were waited for; matrix products, arithmetic and copies ran while one was open for 18% of the time, Pallas kernels for 0%

profile of v1, /device:TPU:0, one launch (start us, length us, event | category | flops | bytes accessed | tf_op | source)
XLA Modules:
  0.0 261.0 jit_solution(12942910886287704054)
XLA Ops:
  8.0 66.3 %all-gather.5.cloned.1.call-done = bf16[2048,512]{1,0:T(8,128)(2,1)} async-done(((bf16[128,512]{1,0:T(8,128)(2,1)}), bf16[2048,512]{1,0:T(8,128)(2,1)}) %all-gather.5.cloned.1.call-update) | async-done | bytes 2097168 | tf_op jit(solution)/shard_map/all_gather | solution.py:37
  77.1 1.5 iota_compare_fusion.1
  78.6 1.3 convert_reduce_fusion.2
  80.4 1.3 broadcast_compare_fusion
  81.7 6.6 %copy.70 = bf16[1024,2048]{0,1:T(8,128)(2,1)} copy(bf16[1024,2048]{1,0:T(8,128)(2,1)} %param.12) | data formatting | bytes 8388608 | tf_op args[1]
  88.3 4.1 %fusion.87 = (bf16[1024,4,1,128]{0,3,2,1:T(8,128)(2,1)S(1)}, bf16[1024,4,1,128]{0,3,2,1:T(8,128)(2,1)S(1)}, bf16[1024,4,1,128]{0,3,2,1:T(8,128)(2,1)}, bf16[1024,4,1,128]{0,3,2,1:T(8,128)(2,1)}) fusion(bf16[1024,4,4,128]{0,3,2,1:T(8,128)(2,1)} %bitcast.133), kind=kLoop, calls=%fused_computation.157 | loop fusion | bytes 8388608 | tf_op jit(solution)/shard_map/slice | solution.py:72
  92.5 2.9 %fusion.92 = f32[512,512]{1,0:T(8,128)} fusion(bf16[512,1024]{1,0:T(8,128)(2,1)S(1)} %copy-done, bf16[1024,512]{1,0:T(8,128)(2,1)} %param.16), kind=kOutput, calls=%fused_computation.162 | convolution fusion | flops 536870912 | bytes 3145728 | tf_op jit(solution)/shard_map/dot_general | solution.py:33
  95.4 3.2 %convert_reduce_fusion = f32[2048]{0:T(1024)S(1)} fusion(bf16[2048,1024]{1,0:T(8,128)(2,1)} %all-gather.7.cloned.1.call-done), kind=kLoop, calls=%fused_computation.1 | loop fusion | flops 4192256 | bytes 4202496 | tf_op jit(solution)/shard_map/reduce_sum | solution.py:19
  99.3 1.4 fusion.2
  100.7 1.1 fusion.3
  103.9 4.7 %multiply_convert_fusion = (bf16[2048,512]{0,1:T(8,128)(2,1)S(1)}, f32[2048,512]{0,1:T(8,128)}) fusion(bf16[2048,1024]{1,0:T(8,128)(2,1)S(1)} %fusion.3, bf16[1024,512]{0,1:T(8,128)(2,1)S(1)} %bitcast.140), kind=kOutput, calls=%fused_computation.24 | convolution fusion | flops 2152726528 | bytes 11534336 | tf_op jit(solution)/shard_map/dot_general | solution.py:33
  108.6 4.7 %multiply_convert_fusion.1 = (bf16[2048,512]{0,1:T(8,128)(2,1)S(1)}, f32[2048,512]{0,1:T(8,128)}) fusion(bf16[2048,1024]{1,0:T(8,128)(2,1)S(1)} %fusion.3, bf16[1024,512]{0,1:T(8,128)(2,1)S(1)} %bitcast.138), kind=kOutput, calls=%fused_computation.26 | convolution fusion | flops 2152726528 | bytes 11534336 | tf_op jit(solution)/shard_map/dot_general | solution.py:33
  113.4 2.5 select_convert_fusion
  119.9 4.6 %psum.28 = f32[4,1024]{1,0:T(4,128)} all-reduce(f32[4,1024]{1,0:T(4,128)} %fusion.73), channel_id=1, replica_groups=mesh['ctx'=16,'cand'=2] {'cand'}, use_global_device_ids=true, to_apply=%region_4.5 | all-reduce | flops 4096 | bytes 32768 | tf_op jit(solution)/shard_map/psum | solution.py:109
  124.5 3.8 %fusion.23 = f32[64,1024]{1,0:T(8,128)} fusion(bf16[2048,1024]{1,0:T(8,128)(2,1)} %all-gather.7.cloned.1.call-done, s32[64]{0:T(128)} %param.18), kind=kOutput, calls=%fused_computation.58 | convolution fusion | flops 268566528 | bytes 4456704 | tf_op jit(solution)/shard_map/dot_general | solution.py:33
  128.3 1.5 fusion.72
  129.8 2.7 %fusion.8 = f32[4,512]{1,0:T(4,128)S(1)} fusion(f32[512]{0:T(512)} %param.17, f32[512,512]{1,0:T(8,128)} %fusion.92, f32[4,512]{1,0:T(4,128)S(1)} %fusion.72), kind=kLoop, calls=%fused_computation.13 | loop fusion | flops 7337984 | bytes 1067008 | tf_op jit(solution)/shard_map/reduce_sum | solution.py:117
  132.6 2.7 %select_reduce_fusion.1 = f32[4,512]{1,0:T(4,128)} fusion(f32[4,512]{1,0:T(4,128)S(1)} %fusion.8, s32[4,512]{1,0:T(4,128)S(1)} %copy-done.27, pred[4,512]{1,0:T(4,128)(4,1)} %broadcast_compare_fusion), kind=kLoop, calls=%fused_computation.23 | loop fusion | flops 4192256 | bytes 26624 | tf_op jit(solution)/shard_map/reduce_sum | solution.py:118
  135.2 2.6 psum.29
  139.9 1.9 select_reduce_fusion
  141.8 2.8 %fusion.12 = f32[4,512]{1,0:T(4,128)S(1)} fusion(f32[4,512]{1,0:T(4,128)S(1)} %select_reduce_fusion, f32[512,512]{1,0:T(8,128)} %fusion.92, f32[4,512]{1,0:T(4,128)} %copy-done.32), kind=kLoop, calls=%fused_computation.17 | loop fusion | flops 10483712 | bytes 1073152 | tf_op jit(solution)/shard_map/reduce_sum | solution.py:125
  144.5 1.3 broadcast_multiply_fusion
  145.8 2.6 psum.30
  148.4 40.8 %all-gather = f32[16,4,512]{2,1,0:T(4,128)} all-gather(f32[1,4,512]{2,1,0:T(4,128)S(1)} %bitcast.146), channel_id=1, replica_groups=mesh['ctx'=16,'cand'=2] {'ctx'}, dimensions={0}, use_global_device_ids=true | all-gather | bytes 139264 | tf_op jit(solution)/shard_map/all_gather | solution.py:42
  189.2 1.6 reshape.150
  190.8 1.2 fusion.64
  192.0 2.3 fusion.93
  194.3 2.4 convolution_bitcast_fusion
  197.2 3.6 %fusion.18 = bf16[4,64,2048]{2,1,0:T(8,128)(2,1)S(1)} fusion(bf16[64,4,128]{2,0,1:T(8,128)(2,1)S(1)} %get-tuple-element.16, bf16[2048,4,128]{0,2,1:T(8,128)(2,1)} %bitcast.145, f32[4,64,2048]{2,1,0:T(8,128)} %get-tuple-element.24, f32[64]{0:T(128)} %copy-done.35, pred[64,2048]{1,0:T(8,128)(4,1)} %iota_compare_fusion.1), kind=kOutput, calls=%fused_computation.35 | convolution fusion | flops 139984896 | bytes 5439744 | tf_op jit(solution)/shard_map/qhd,khd->hqk/dot_general | solution.py:144
  202.5 2.7 %fusion.94 = f32[4,128,2048]{2,1,0:T(8,128)} fusion(bf16[64,4,128]{2,0,1:T(8,128)(2,1)S(1)} %get-tuple-element.16, bf16[4,64,2048]{2,1,0:T(8,128)(2,1)S(1)} %copy-done.6), kind=kOutput, calls=%fused_computation.164 | convolution fusion | flops 134217728 | bytes 5308416 | tf_op jit(solution)/shard_map/hqk,qhd->khd/dot_general | solution.py:148
  205.3 1.1 convert_reduce_fusion.1
  207.1 1.5 fusion.14
  208.6 1.1 fusion.37
  209.8 2.8 %fusion.24 = f32[64,512]{1,0:T(8,128)} fusion(bf16[2048,512]{0,1:T(8,128)(2,1)S(1)} %fusion.14, bf16[2048,1024]{1,0:T(8,128)(2,1)} %copy-done.2, s32[]{:T(128)S(6)} %select_n.40), kind=kOutput, calls=%fused_computation.59 | convolution fusion | flops 134217728 | bytes 2752516 | tf_op jit(solution)/shard_map/dot_general | solution.py:159
  214.4 1.6 stack_reshape.14
  216.0 1.6 stack_reshape.12
  217.5 1.6 stack_reshape.15
  219.1 5.0 %fusion.13 = bf16[2048,512]{0,1:T(8,128)(2,1)S(1)} fusion(f32[4,128,2048]{2,1,0:T(8,128)} %fusion.94, f32[2048,512]{0,1:T(8,128)} %get-tuple-element.20), kind=kLoop, calls=%fused_computation.19 | loop fusion | flops 9437184 | bytes 10485760 | tf_op jit(solution)/shard_map/convert_element_type | solution.py:151
  224.2 2.8 %fusion.26 = f32[64,512]{1,0:T(8,128)} fusion(bf16[2048,512]{0,1:T(8,128)(2,1)S(1)} %fusion.13, bf16[2048,1024]{1,0:T(8,128)(2,1)} %copy-done.2, s32[]{:T(128)S(6)} %select_n.40), kind=kOutput, calls=%fused_computation.61 | convolution fusion | flops 134217728 | bytes 2752516 | tf_op jit(solution)/shard_map/dot_general | solution.py:159
  227.0 1.1 convolution_add_fusion.2
  228.2 2.3 convolution_add_fusion.1
  230.5 2.4 convolution_add_fusion
  233.8 1.2 pad_maximum_fusion
  236.4 1.2 fusion.22
  237.5 1.0 fusion.51
  238.6 12.5 %all-reduce.2.cloned.1.call-done = f32[128,1024]{1,0:T(8,128)} async-done(((f32[128,1024]{1,0:T(8,128)}), f32[128,1024]{1,0:T(8,128)}) %all-reduce.2.cloned.1.call-update) | async-done | bytes 524304 | tf_op jit(solution)/shard_map/psum | solution.py:184
  251.1 1.3 fusion.86
  252.5 2.0 convolution_add_fusion.3
  (116 shorter events, 19.9 us)
Async XLA Ops:
  7.2 85.3 %copy-start = (bf16[512,1024]{1,0:T(8,128)(2,1)S(1)}, bf16[512,1024]{1,0:T(8,128)(2,1)}, u32[]{:S(2)}) copy-start(bf16[512,1024]{1,0:T(8,128)(2,1)} %param.14) | copy-start | bytes 3145732
  7.2 67.0 %all-gather.5.cloned.1.call-start = ((), (), s32[]{:S(2)}) async-start(), calls=%async_computation | async-start | bytes 2228224 | tf_op jit(solution)/shard_map/all_gather | solution.py:37
  7.9 87.5 %all-gather.7.cloned.1.call-start = ((), (), s32[]{:S(2)}) async-start(), calls=%async_computation.1 | async-start | bytes 6291456 | tf_op jit(solution)/shard_map/all_gather | solution.py:38
  74.2 54.1 %all-gather.9.cloned.1.call-start = ((), (), s32[]{:S(2)}) async-start(), calls=%async_computation.2 | async-start | bytes 1572864 | tf_op jit(solution)/shard_map/all_gather | solution.py:75
  75.0 176.1 %all-reduce.2.cloned.1.call-start = ((), (), s32[]{:S(2)}) async-start(), calls=%async_computation.3 | async-start | bytes 1048576 | tf_op jit(solution)/shard_map/psum | solution.py:184
  76.2 37.2 %copy-start.35 = (f32[64]{0:T(128)}, f32[64]{0:T(128)S(1)}, u32[]{:S(2)}) copy-start(f32[64]{0:T(128)S(1)} %add_convert_fusion.2) | copy-start | bytes 772
  95.4 4.0 %copy-start.1 = (bf16[2048,1024]{1,0:T(8,128)(2,1)S(1)}, bf16[2048,1024]{1,0:T(8,128)(2,1)}, u32[]{:S(2)}) copy-start(bf16[2048,1024]{1,0:T(8,128)(2,1)} %all-gather.7.cloned.1.call-done) | copy-start | bytes 12582916
  100.7 1.1 copy-start.30
  101.9 6.7 %copy-start.2 = (bf16[2048,1024]{1,0:T(8,128)(2,1)}, bf16[2048,1024]{1,0:T(8,128)(2,1)S(1)}, u32[]{:S(2)}) copy-start(bf16[2048,1024]{1,0:T(8,128)(2,1)S(1)} %fusion.3) | copy-start | bytes 12582916
  101.9 2.0 copy-start.9
  103.7 9.7 %copy-start.17 = (f32[64,512]{1,0:T(8,128)}, f32[64,512]{1,0:T(8,128)S(1)}, u32[]{:S(2)}) copy-start(f32[64,512]{1,0:T(8,128)S(1)} %fusion.90) | copy-start | bytes 393220
  103.9 4.7 %copy-start.7 = (bf16[1024,4,1,128]{0,3,2,1:T(8,128)(2,1)S(1)}, bf16[1024,4,1,128]{0,3,2,1:T(8,128)(2,1)}, u32[]{:S(2)}) copy-start(bf16[1024,4,1,128]{0,3,2,1:T(8,128)(2,1)} %get-tuple-element.14) | copy-start | bytes 3145732
  108.6 4.8 %copy-start.12 = (bf16[2048,512]{0,1:T(8,128)(2,1)}, bf16[2048,512]{0,1:T(8,128)(2,1)S(1)}, u32[]{:S(2)}) copy-start(bf16[2048,512]{0,1:T(8,128)(2,1)S(1)} %get-tuple-element.21) | copy-start | bytes 6291460
  108.6 4.8 %copy-start.23 = (pred[64,2048]{1,0:T(8,128)(4,1)S(1)}, pred[64,2048]{1,0:T(8,128)(4,1)}, u32[]{:S(2)}) copy-start(pred[64,2048]{1,0:T(8,128)(4,1)} %iota_compare_fusion.1) | copy-start | bytes 393220
  113.4 2.5 copy-start.14
  113.4 5.6 %copy-start.4 = (bf16[512,1024]{1,0:T(8,128)(2,1)S(1)}, bf16[512,1024]{1,0:T(8,128)(2,1)}, u32[]{:S(2)}) copy-start(bf16[512,1024]{1,0:T(8,128)(2,1)} %param.13) | copy-start | bytes 3145732
  115.9 1.0 copy-start.5
  117.9 0.6 copy-start.25
  118.5 0.6 copy-start.28
  119.1 13.5 %copy-start.27 = (s32[4,512]{1,0:T(4,128)S(1)}, s32[4,512]{1,0:T(4,128)}, u32[]{:S(2)}) copy-start(s32[4,512]{1,0:T(4,128)} %param.20) | copy-start | bytes 24580
  119.1 18.7 %copy-start.24 = (s32[4,512]{1,0:T(4,128)S(1)}, s32[4,512]{1,0:T(4,128)}, u32[]{:S(2)}) copy-start(s32[4,512]{1,0:T(4,128)} %param.21) | copy-start | bytes 24580
  129.8 2.7 %copy-start.32 = (f32[4,512]{1,0:T(4,128)}, f32[4,512]{1,0:T(4,128)S(1)}, u32[]{:S(2)}) copy-start(f32[4,512]{1,0:T(4,128)S(1)} %fusion.72) | copy-start | bytes 24580
  139.8 56.9 %copy-start.26 = (f32[64,4]{0,1:T(4,128)S(1)}, f32[64,4]{0,1:T(4,128)}, u32[]{:S(2)}) copy-start(f32[64,4]{0,1:T(4,128)} %copy-done.25) | copy-start | bytes 3076
  139.8 56.9 %copy-start.29 = (f32[64,4]{0,1:T(4,128)S(1)}, f32[64,4]{0,1:T(4,128)}, u32[]{:S(2)}) copy-start(f32[64,4]{0,1:T(4,128)} %copy-done.28) | copy-start | bytes 3076
  194.3 2.9 %copy-start.15 = (f32[64,1024]{1,0:T(8,128)}, f32[64,1024]{1,0:T(8,128)S(1)}, u32[]{:S(2)}) copy-start(f32[64,1024]{1,0:T(8,128)S(1)} %fusion.93) | copy-start | bytes 786436
  197.2 3.7 %copy-start.13 = (bf16[2048,512]{0,1:T(8,128)(2,1)S(1)}, bf16[2048,512]{0,1:T(8,128)(2,1)}, u32[]{:S(2)}) copy-start(bf16[2048,512]{0,1:T(8,128)(2,1)} %copy-done.12) | copy-start | bytes 6291460
  197.2 4.5 %copy-start.18 = (f32[64,512]{1,0:T(8,128)S(1)}, f32[64,512]{1,0:T(8,128)}, u32[]{:S(2)}) copy-start(f32[64,512]{1,0:T(8,128)} %copy-done.17) | copy-start | bytes 393220
  200.9 1.6 copy-start.6
  202.5 4.6 %copy-start.3 = (f32[2048,512]{0,1:T(8,128)S(1)}, f32[2048,512]{0,1:T(8,128)}, u32[]{:S(2)}) copy-start(f32[2048,512]{0,1:T(8,128)} %get-tuple-element.22) | copy-start | bytes 12582916
  207.0 6.5 %copy-start.19 = (bf16[64,512]{1,0:T(8,128)(2,1)}, bf16[64,512]{1,0:T(8,128)(2,1)S(1)}, u32[]{:S(2)}) copy-start(bf16[64,512]{1,0:T(8,128)(2,1)S(1)} %fusion.33) | copy-start | bytes 196612
  207.1 5.5 %copy-start.21 = (bf16[64,512]{1,0:T(8,128)(2,1)}, bf16[64,512]{1,0:T(8,128)(2,1)S(1)}, u32[]{:S(2)}) copy-start(bf16[64,512]{1,0:T(8,128)(2,1)S(1)} %fusion.32) | copy-start | bytes 196612
  207.1 1.5 copy-start.10
  219.1 7.9 %copy-start.8 = (bf16[1024,4,1,128]{0,3,2,1:T(8,128)(2,1)S(1)}, bf16[1024,4,1,128]{0,3,2,1:T(8,128)(2,1)}, u32[]{:S(2)}) copy-start(bf16[1024,4,1,128]{0,3,2,1:T(8,128)(2,1)} %get-tuple-element.14) | copy-start | bytes 3145732
  219.1 7.9 %copy-start.11 = (f32[128,1024]{1,0:T(8,128)S(1)}, f32[128,1024]{1,0:T(8,128)}, u32[]{:S(2)}) copy-start(f32[128,1024]{1,0:T(8,128)} %fusion.37) | copy-start | bytes 1572868
  224.2 4.0 %copy-start.20 = (bf16[64,512]{1,0:T(8,128)(2,1)S(1)}, bf16[64,512]{1,0:T(8,128)(2,1)}, u32[]{:S(2)}) copy-start(bf16[64,512]{1,0:T(8,128)(2,1)} %copy-done.19) | copy-start | bytes 196612
  224.2 4.0 %copy-start.31 = (s32[64]{0:T(128)S(1)}, s32[64]{0:T(128)}, u32[]{:S(2)}) copy-start(s32[64]{0:T(128)} %param.18) | copy-start | bytes 772
  224.2 4.0 %copy-start.33 = (s32[128]{0:T(128)S(1)}, s32[128]{0:T(128)}, u32[]{:S(2)}) copy-start(s32[128]{0:T(128)} %iota_add_fusion) | copy-start | bytes 1540
  224.2 6.3 %copy-start.22 = (bf16[64,512]{1,0:T(8,128)(2,1)S(1)}, bf16[64,512]{1,0:T(8,128)(2,1)}, u32[]{:S(2)}) copy-start(bf16[64,512]{1,0:T(8,128)(2,1)} %copy-done.21) | copy-start | bytes 196612
  230.5 5.8 %copy-start.34 = (f32[128]{0:T(128)S(1)}, f32[128]{0:T(128)}, u32[]{:S(2)}) copy-start(f32[128]{0:T(128)} %broadcast_multiply_fusion.7) | copy-start | bytes 1540
  230.5 7.0 %copy-start.16 = (f32[64,1024]{1,0:T(8,128)S(1)}, f32[64,1024]{1,0:T(8,128)}, u32[]{:S(2)}) copy-start(f32[64,1024]{1,0:T(8,128)} %copy-done.15) | copy-start | bytes 786436
Sparse Core Ops, SparseCore 0:
  10.8 63.3 all-gather.4
  75.8 12.3 all-gather.6
  89.7 10.1 all-gather.8
  236.5 14.5 all-reduce.1

commit v2 on v1

--- a/solution.py
+++ b/solution.py
@@ -1,6 +1,10 @@
+import functools
+
 import jax
 import jax.numpy as jnp
 from jax import lax
+from jax.experimental import pallas as pl
+from jax.experimental.pallas import tpu as pltpu
 from jax.sharding import PartitionSpec as P
 
 HEAD = 128
@@ -33,13 +37,308 @@
     return jnp.dot(left, right, preferred_element_type=F32)
 
 
-def gather_history(history):
-    rows = lax.all_gather(history, "ctx", axis=0, tiled=True)
-    return lax.all_gather(rows, "cand", axis=1, tiled=True)
+MESH = pl.DeviceIdType.MESH
+VMEM = pl.BlockSpec(memory_space=pltpu.VMEM)
+DMA = pltpu.SemaphoreType.DMA
+
+
+def kernel_params(collective_id):
+    return pltpu.CompilerParams(
+        collective_id=collective_id, has_side_effects=True, vmem_limit_bytes=48 * 1024 * 1024
+    )
+
+
+def flip(number, bits):
+    place = 1
+    result = number
+    while place <= bits:
+        if bits & place:
+            result = result + place - 2 * place * ((number // place) % 2)
+        place *= 2
+    return result
+
+
+def meet(peers):
+    barrier = pltpu.get_barrier_semaphore()
+    for peer in peers:
+        pl.semaphore_signal(barrier, inc=1, device_id=peer, device_id_type=MESH)
+    pl.semaphore_wait(barrier, len(peers))
+
+
+def history_kernel(
+    ctx_count,
+    cand_count,
+    history,
+    user,
+    features,
+    user_full,
+    line_send,
+    first_send,
+    second_send,
+    cand_send,
+    ctx_recv,
+    cand_recv,
+    user_send,
+    user_recv,
+):
+    rows, slice_width = history.shape
+    user_rows = user.shape[0]
+    ctx = lax.axis_index("ctx")
+    cand = lax.axis_index("cand")
+    depth = ctx_count // 4
+    line, low = ctx // 4, ctx % 4
+    odd = cand % 2
+    flip_x, flip_y = flip(ctx, 1), flip(ctx, 2)
+    first = flip_x + odd * (flip_y - flip_x)
+    second = flip_y + odd * (flip_x - flip_y)
+    line_peers = [flip(line, step) * 4 + low for step in range(1, depth)]
+    cand_peers = [(cand + step) % cand_count for step in range(1, cand_count)]
+    meet(
+        [(peer, cand) for peer in line_peers]
+        + [(first, cand), (second, cand)]
+        + [(ctx, peer) for peer in cand_peers]
+    )
+    columns = pl.ds(pl.multiple_of(cand * slice_width, slice_width), slice_width)
+
+    def place(block):
+        return features.at[pl.ds(pl.multiple_of(block * rows, rows), rows), columns]
+
+    pending = []
+
+    def send(source, block, send_sem, recv_sem, peer):
+        copy = pltpu.make_async_remote_copy(
+            src_ref=source,
+            dst_ref=place(block),
+            send_sem=send_sem,
+            recv_sem=recv_sem,
+            device_id=peer,
+            device_id_type=MESH,
+        )
+        copy.start()
+        pending.append(copy)
+
+    def arrive(block):
+        pltpu.make_async_remote_copy(
+            src_ref=place(block),
+            dst_ref=place(block),
+            send_sem=line_send.at[0],
+            recv_sem=ctx_recv.at[block],
+            device_id=(ctx, cand),
+            device_id_type=MESH,
+        ).wait_recv()
+
+    def share(source, block, slot):
+        for step, peer in enumerate(cand_peers):
+            send(
+                source, block, cand_send.at[slot, step], cand_recv.at[block, step], (ctx, peer)
+            )
+
+    for step, peer in enumerate(line_peers):
+        send(history, ctx, line_send.at[step], ctx_recv.at[ctx], (peer, cand))
+    send(history, ctx, first_send.at[0], ctx_recv.at[ctx], (first, cand))
+    send(history, ctx, second_send.at[0], ctx_recv.at[ctx], (second, cand))
+    share(history, ctx, 0)
+    own_user = pl.ds(pl.multiple_of(cand * user_rows, user_rows), user_rows)
+    for step, peer in enumerate(cand_peers):
+        copy = pltpu.make_async_remote_copy(
+            src_ref=user,
+            dst_ref=user_full.at[own_user],
+            send_sem=user_send.at[step],
+            recv_sem=user_recv.at[step],
+            device_id=(ctx, peer),
+            device_id_type=MESH,
+        )
+        copy.start()
+        pending.append(copy)
+    user_full[own_user, :] = user[...]
+    features[pl.ds(pl.multiple_of(ctx * rows, rows), rows), columns] = history[...]
+
+    for step in range(depth):
+        if step > 0:
+            block = flip(line, step) * 4 + low
+            arrive(block)
+            send(place(block), block, first_send.at[step], ctx_recv.at[block], (first, cand))
+            send(place(block), block, second_send.at[step], ctx_recv.at[block], (second, cand))
+            share(place(block), block, step)
+        block = flip(line, step) * 4 + first % 4
+        arrive(block)
+        send(place(block), block, second_send.at[depth + step], ctx_recv.at[block], (second, cand))
+        share(place(block), block, depth + step)
+    for step in range(depth):
+        for part, corner in enumerate((second % 4, 3 - low)):
+            block = flip(line, step) * 4 + corner
+            arrive(block)
+            share(place(block), block, (2 + part) * depth + step)
+    for step in range(1, cand_count):
+        source = (cand + cand_count - step) % cand_count
+        there = pl.ds(pl.multiple_of(source * slice_width, slice_width), slice_width)
+        user_there = pl.ds(pl.multiple_of(source * user_rows, user_rows), user_rows)
+        for block in range(ctx_count):
+            landed = features.at[pl.ds(block * rows, rows), there]
+            pltpu.make_async_remote_copy(
+                src_ref=landed,
+                dst_ref=landed,
+                send_sem=cand_send.at[0, 0],
+                recv_sem=cand_recv.at[block, step - 1],
+                device_id=(ctx, cand),
+                device_id_type=MESH,
+            ).wait_recv()
+        pltpu.make_async_remote_copy(
+            src_ref=user_full.at[user_there],
+            dst_ref=user_full.at[user_there],
+            send_sem=user_send.at[0],
+            recv_sem=user_recv.at[step - 1],
+            device_id=(ctx, cand),
+            device_id_type=MESH,
+        ).wait_recv()
+    for copy in pending:
+        copy.wait_send()
+
+
+def gather_history(history, user_weights):
+    ctx_count, cand_count = lax.axis_size("ctx"), lax.axis_size("cand")
+    rows, slice_width = history.shape
+    user_rows, hidden = user_weights.shape
+    depth = ctx_count // 4
+    others = cand_count - 1
+    return pl.pallas_call(
+        functools.partial(history_kernel, ctx_count, cand_count),
+        out_shape=(
+            jax.ShapeDtypeStruct((rows * ctx_count, slice_width * cand_count), history.dtype),
+            jax.ShapeDtypeStruct((user_rows * cand_count, hidden), user_weights.dtype),
+        ),
+        in_specs=[VMEM, VMEM],
+        out_specs=(VMEM, VMEM),
+        scratch_shapes=[
+            DMA((max(depth - 1, 1),)),
+            DMA((depth,)),
+            DMA((2 * depth,)),
+            DMA((ctx_count, others)),
+            DMA((ctx_count,)),
+            DMA((ctx_count, others)),
+            DMA((others,)),
+            DMA((others,)),
+        ],
+        compiler_params=kernel_params(0),
+        name="history_gather",
+    )(history, user_weights)
+
+
+def swap_cores(cand_count, source, slots, send_sem, recv_sem):
+    ctx = lax.axis_index("ctx")
+    cand = lax.axis_index("cand")
+    copies = []
+    for step in range(1, cand_count):
+        copy = pltpu.make_async_remote_copy(
+            src_ref=source,
+            dst_ref=slots.at[step - 1],
+            send_sem=send_sem.at[step - 1],
+            recv_sem=recv_sem.at[step - 1],
+            device_id=(ctx, (cand + step) % cand_count),
+            device_id_type=MESH,
+        )
+        copy.start()
+        copies.append(copy)
+    return copies
+
+
+def ordered_sum(cand_count, own, slots):
+    cand = lax.axis_index("cand")
+    total = None
+    for owner in range(cand_count):
+        term = own[...]
+        for step in range(1, cand_count):
+            term = jnp.where((owner + step) % cand_count == cand, slots[step - 1], term)
+        total = term if total is None else total + term
+    return total
+
+
+def user_grad_kernel(
+    ctx_count, cand_count, part, out, slots, core_send, core_recv, send_sem, recv_sem
+):
+    ctx = lax.axis_index("ctx")
+    cand = lax.axis_index("cand")
+    ctx_peers = [(ctx + step) % ctx_count for step in range(1, ctx_count)]
+    meet(
+        [(ctx, (cand + step) % cand_count) for step in range(1, cand_count)]
+        + [(peer, cand) for peer in ctx_peers]
+    )
+    copies = swap_cores(cand_count, part, slots, core_send, core_recv)
+    for copy in copies:
+        copy.wait()
+    out[ctx] = ordered_sum(cand_count, part, slots)
+    copies = []
+    for step, peer in enumerate(ctx_peers):
+        copy = pltpu.make_async_remote_copy(
+            src_ref=out.at[ctx],
+            dst_ref=out.at[ctx],
+            send_sem=send_sem.at[step],
+            recv_sem=recv_sem.at[step],
+            device_id=(peer, cand),
+            device_id_type=MESH,
+        )
+        copy.start()
+        copies.append(copy)
+    for step, copy in enumerate(copies):
+        source = (ctx + ctx_count - step - 1) % ctx_count
+        pltpu.make_async_remote_copy(
+            src_ref=out.at[source],
+            dst_ref=out.at[source],
+            send_sem=send_sem.at[step],
+            recv_sem=recv_sem.at[step],
+            device_id=(ctx, cand),
+            device_id_type=MESH,
+        ).wait_recv()
+    for copy in copies:
+        copy.wait_send()
 
 
 def gather_user_grad(part):
-    return lax.all_gather(lax.psum(part, "cand"), "ctx", axis=0, tiled=True)
+    ctx_count, cand_count = lax.axis_size("ctx"), lax.axis_size("cand")
+    others = cand_count - 1
+    gathered = pl.pallas_call(
+        functools.partial(user_grad_kernel, ctx_count, cand_count),
+        out_shape=jax.ShapeDtypeStruct((ctx_count,) + part.shape, F32),
+        in_specs=[VMEM],
+        out_specs=VMEM,
+        scratch_shapes=[
+            pltpu.VMEM((others,) + part.shape, F32),
+            DMA((others,)),
+            DMA((others,)),
+            DMA((ctx_count - 1,)),
+            DMA((ctx_count - 1,)),
+        ],
+        compiler_params=kernel_params(1),
+        name="user_grad_gather",
+    )(part)
+    return gathered.reshape(ctx_count * part.shape[0], part.shape[1])
+
+
+def core_sum_kernel(cand_count, part, out, slots, send_sem, recv_sem):
+    ctx = lax.axis_index("ctx")
+    cand = lax.axis_index("cand")
+    meet([(ctx, (cand + step) % cand_count) for step in range(1, cand_count)])
+    for copy in swap_cores(cand_count, part, slots, send_sem, recv_sem):
+        copy.wait()
+    out[...] = ordered_sum(cand_count, part, slots)
+
+
+def core_sum(part, collective_id):
+    cand_count = lax.axis_size("cand")
+    others = cand_count - 1
+    return pl.pallas_call(
+        functools.partial(core_sum_kernel, cand_count),
+        out_shape=jax.ShapeDtypeStruct(part.shape, F32),
+        in_specs=[VMEM],
+        out_specs=VMEM,
+        scratch_shapes=[
+            pltpu.VMEM((others,) + part.shape, F32),
+            DMA((others,)),
+            DMA((others,)),
+        ],
+        compiler_params=kernel_params(collective_id),
+        name="core_sum",
+    )(part)
 
 
 def per_device(
@@ -72,9 +371,7 @@
         sections[:, :, index].reshape(width, cols) for index in range(4)
     )
     item_proj = mm(cand_table, item_weights)
-    user_full = lax.all_gather(user_weights, "cand", axis=0, tiled=True)
-
-    features = gather_history(history)
+    features, user_full = gather_history(history, user_weights)
     length = features.shape[0]
     x_low = layer_norm(features.astype(F32))[0].astype(BF16)
 
@@ -181,12 +478,12 @@
     def back(grads, weights):
         return lax.dot_general(grads, weights, transposed, preferred_element_type=F32)
 
-    d_normed = lax.psum(
+    d_normed = core_sum(
         back(own_rows(d_before_key), key_w)
         + back(own_rows(d_before_value), value_w)
         + back(mm(low_places, d_before_query).astype(BF16), query_w)
         + back(mm(low_places, d_before_gate).astype(BF16), gate_w),
-        "cand",
+        2,
     )
     x_normed, x_inverse = layer_norm(own_rows(features).astype(F32))
     column_start = cand_index * slice_width

time: 262 us -> 141 us (0.54)
  waiting for transfers between devices: 80.2 us -> 0 us
  blocking collectives: 50.6 us -> 6.1 us
  Pallas kernels: 0 us -> 43.8 us
  between operations: 14.3 us -> 1.28 us
  other arithmetic: 38.4 us -> 26.3 us
  matrix products: 55 us -> 44.8 us
  local copies, waits for them, and re-layouts: 22.3 us -> 17.7 us
    all_gather x3 -> x0, waiting for transfers between devices: 66.3 us -> none  [the longest x1 66.3 us: gather_history(): rows = lax.all_gather(history, 'ctx', axis=0, tiled=True)]
    pallas_call x0 -> x3, Pallas kernels: none -> 43.8 us  [the longest x1 33.3 us: gather_history(): pl.pallas_call(functools.partial(history_kernel, ctx_count, cand_count),...]
    all_gather x1 -> x0, blocking collectives: 40.8 us -> none  [gather_user_grad(): return lax.all_gather(lax.psum(part, 'cand'), 'ctx', axis=0, tiled=True)]
    psum x1 -> x0, waiting for transfers between devices: 12.5 us -> none  [per_device(): lax.psum(back(own_rows(d_before_key), key_w) + back(own_rows(d_before_val...]
    convert_element_type x1, other arithmetic: 5.02 us -> 1.51 us  [per_device(): (d_value.reshape(length, cols) * silu_slope(before_value)).astype(BF16)]
    reduce_sum x2, other arithmetic: 4.23 us -> 0.74 us  [layer_norm(): centred = argument - jnp.mean(argument, -1, keepdims=True)]
    dot_general x9, matrix products: 20.3 us -> 17 us  [mm(): return jnp.dot(left, right, preferred_element_type=F32)]
    another operation x5, local copies, waits for them, and re-layouts: 6.05 us -> 3.37 us  [per_device(): jnp.stack([grad_of(x_own_requests, d_before_gate), grad_of(x_own, d_befor...]
  transfers between devices with their start and end apart: 4 -> 0, of which waited for: 2 -> 0; matrix products, arithmetic and copies ran while one was open for 18% -> 0% of each run, Pallas kernels for 0% -> 0%
where the time goes in v2:
time: 141 us; the launch traced here: 140 us
  matrix products  44.8 us (32%)
  Pallas kernels  43.8 us (31%)
  other arithmetic  26.3 us (19%)
  local copies, waits for them, and re-layouts  17.7 us (13%)
  blocking collectives  6.1 us (4%)
    pallas_call x1, Pallas kernels, gather_history(): pl.pallas_call(functools.partial(history_kernel, ctx_count, cand_count),...  33.3 us
    dot_general x9, matrix products, mm(): return jnp.dot(left, right, preferred_element_type=F32)  17 us
    unnamed x87, local copies, waits for them, and re-layouts  9.81 us
    pallas_call x1, Pallas kernels, gather_user_grad(): pl.pallas_call(functools.partial(user_grad_kernel, ctx_count, cand_count)...  8.54 us
    dot_general x4, matrix products, grad_of(): lax.dot_general(rows, grads, (((0,), (0,)), ((), ())), preferred_element_...  6.95 us
    dot_general x4, matrix products, back(): lax.dot_general(grads, weights, transposed, preferred_element_type=F32)  6.16 us
    psum x1, blocking collectives, per_device(): head_total = lax.psum(mm(own(gated), merge_weights), 'cand')  3.6 us
    another operation x5, local copies, waits for them, and re-layouts, per_device(): jnp.stack([grad_of(x_own_requests, d_before_gate), grad_of(x_own, d_befor...  3.37 us

profile of v2, /device:TPU:0, one launch (start us, length us, event | category | flops | bytes accessed | tf_op | source)
XLA Modules:
  0.0 140.1 jit_solution(18142290532854641666)
XLA Ops:
  1.2 1.3 convert_reduce_fusion.2
  2.5 1.2 add_convert_fusion.2
  3.7 0.9 fusion.63
  6.7 3.0 %fusion.92 = f32[512,512]{1,0:T(8,128)} fusion(bf16[512,1024]{1,0:T(8,128)(2,1)S(1)} %copy-done, bf16[1024,512]{1,0:T(8,128)(2,1)} %param.16), kind=kOutput, calls=%fused_computation.162 | convolution fusion | flops 536870912 | bytes 3145728 | tf_op jit(solution)/shard_map/dot_general | solution.py:37
  9.6 6.4 %copy.55 = bf16[1024,2048]{0,1:T(8,128)(2,1)} copy(bf16[1024,2048]{1,0:T(8,128)(2,1)} %param.12) | data formatting | bytes 8388608 | tf_op args[1]
  16.0 2.9 %fusion.87 = (bf16[1024,4,1,128]{0,3,2,1:T(8,128)(2,1)S(1)}, bf16[1024,4,1,128]{0,3,2,1:T(8,128)(2,1)S(1)}, bf16[1024,4,1,128]{0,3,2,1:T(8,128)(2,1)S(1)}, bf16[1024,4,1,128]{0,3,2,1:T(8,128)(2,1)S(1)}) fusion(bf16[1024,4,4,128]{0,3,2,1:T(8,128)(2,1)} %bitcast.132), kind=kLoop, calls=%fused_computation.157 | loop fusion | bytes 8388608 | tf_op jit(solution)/shard_map/slice | solution.py:371
  18.9 33.3 %history_gather.1 = (bf16[2048,1024]{1,0:T(8,128)(2,1)S(1)}, bf16[1024,512]{1,0:T(8,128)(2,1)S(1)}) custom-call(bf16[128,512]{1,0:T(8,128)(2,1)S(1)} %copy-done.3, bf16[512,512]{1,0:T(8,128)(2,1)S(1)} %copy-done.2), custom_call_target="tpu_custom_call" | custom-call | tf_op jit(solution)/shard_map/history_gather/pallas_call | solution.py:204
  52.6 0.8 add_rsqrt_fusion.2
  54.0 1.4 fusion.2
  55.5 1.6 %fusion.23 = f32[64,1024]{1,0:T(8,128)} fusion(bf16[2048,1024]{1,0:T(8,128)(2,1)S(1)} %get-tuple-element.6, s32[64]{0:T(128)S(1)} %copy-done.35), kind=kOutput, calls=%fused_computation.58 | convolution fusion | flops 268566528 | bytes 4456704 | tf_op jit(solution)/shard_map/dot_general | solution.py:37
  57.1 1.1 fusion.3
  58.2 0.9 convolution_convert_fusion
  60.0 4.7 %multiply_convert_fusion = (bf16[2048,512]{0,1:T(8,128)(2,1)S(1)}, f32[2048,512]{0,1:T(8,128)}) fusion(bf16[2048,1024]{1,0:T(8,128)(2,1)S(1)} %fusion.3, bf16[1024,512]{0,1:T(8,128)(2,1)S(1)} %bitcast.139), kind=kOutput, calls=%fused_computation.24 | convolution fusion | flops 2152726528 | bytes 11534336 | tf_op jit(solution)/shard_map/dot_general | solution.py:37
  64.8 2.5 %select_convert_fusion = (bf16[4,64,2048]{2,1,0:T(8,128)(2,1)S(1)}, f32[4,64,2048]{2,1,0:T(8,128)}) fusion(f32[64]{0:T(128)S(1)} %copy-done.41, pred[64,2048]{1,0:T(8,128)(4,1)S(1)} %iota_compare_fusion.1, bf16[2048,4,128]{0,2,1:T(8,128)(2,1)S(1)} %bitcast.141, f32[64,512]{1,0:T(8,128)S(1)} %fusion.90), kind=kOutput, calls=%fused_computation.36 | convolution fusion | flops 138575872 | bytes 5505280 | tf_op jit(solution)/shard_map/qhd,khd->hqk/dot_general | solution.py:395
  67.3 4.7 %multiply_convert_fusion.1 = (bf16[2048,512]{0,1:T(8,128)(2,1)S(1)}, f32[2048,512]{0,1:T(8,128)}) fusion(bf16[2048,1024]{1,0:T(8,128)(2,1)S(1)} %fusion.3, bf16[1024,512]{0,1:T(8,128)(2,1)S(1)} %bitcast.137), kind=kOutput, calls=%fused_computation.26 | convolution fusion | flops 2152726528 | bytes 11534336 | tf_op jit(solution)/shard_map/dot_general | solution.py:37
  72.0 0.9 fusion.89
  73.9 3.6 %psum.14 = f32[4,1024]{1,0:T(4,128)S(1)} all-reduce(f32[4,1024]{1,0:T(4,128)S(1)} %fusion.73), channel_id=1, replica_groups=mesh['ctx'=16,'cand'=2] {'cand'}, use_global_device_ids=true, to_apply=%region_4.5 | all-reduce | flops 4096 | bytes 32768 | tf_op jit(solution)/shard_map/psum | solution.py:406
  77.5 1.0 fusion.72
  78.5 2.7 %fusion.8 = f32[4,512]{1,0:T(4,128)S(1)} fusion(f32[512]{0:T(512)S(1)} %copy-done.40, f32[512,512]{1,0:T(8,128)} %fusion.92, f32[4,512]{1,0:T(4,128)S(1)} %fusion.72), kind=kLoop, calls=%fused_computation.13 | loop fusion | flops 7337984 | bytes 1067008 | tf_op jit(solution)/shard_map/reduce_sum | solution.py:414
  81.2 1.4 select_reduce_fusion.1
  82.6 2.5 %psum.15 = f32[4,512]{1,0:T(4,128)S(1)} all-reduce(f32[4,512]{1,0:T(4,128)S(1)} %select_reduce_fusion.1), channel_id=1, replica_groups=mesh['ctx'=16,'cand'=2] {'cand'}, use_global_device_ids=true, to_apply=%region_7.8 | all-reduce | flops 2048 | bytes 16384 | tf_op jit(solution)/shard_map/psum | solution.py:415
  85.1 0.9 exponential_reduce_fusion
  87.2 1.2 select_reduce_fusion
  88.4 2.8 %fusion.12 = f32[4,512]{1,0:T(4,128)S(1)} fusion(f32[4,512]{1,0:T(4,128)S(1)} %select_reduce_fusion, f32[512,512]{1,0:T(8,128)} %fusion.92, f32[4,512]{1,0:T(4,128)S(1)} %fusion.72), kind=kLoop, calls=%fused_computation.17 | loop fusion | flops 10483712 | bytes 1073152 | tf_op jit(solution)/shard_map/reduce_sum | solution.py:422
  91.9 8.5 %user_grad_gather.1 = f32[16,4,512]{2,1,0:T(4,128)S(1)} custom-call(f32[4,512]{1,0:T(4,128)S(1)} %broadcast_multiply_fusion.part), custom_call_target="tpu_custom_call" | custom-call | tf_op jit(solution)/shard_map/user_grad_gather/pallas_call | solution.py:299
  101.1 1.3 fusion.64
  102.4 1.1 fusion.93
  103.5 2.4 %convolution_bitcast_fusion = f32[8,4,8,128]{3,2,1,0:T(8,128)S(1)} fusion(f32[64,1024]{1,0:T(8,128)S(1)} %fusion.93, bf16[512,1024]{1,0:T(8,128)(2,1)} %param.13), kind=kOutput, calls=%fused_computation.45 | convolution fusion | flops 402653184 | bytes 1441792 | tf_op jit(solution)/shard_map/dot_general | solution.py:431
  106.4 1.0 fusion.51
  107.4 2.1 %fusion.18 = bf16[4,64,2048]{2,1,0:T(8,128)(2,1)S(1)} fusion(bf16[64,4,128]{2,0,1:T(8,128)(2,1)S(1)} %get-tuple-element.20, bf16[2048,4,128]{0,2,1:T(8,128)(2,1)S(1)} %bitcast.144, f32[4,64,2048]{2,1,0:T(8,128)S(1)} %copy-done.42, f32[64]{0:T(128)} %add_convert_fusion.2, pred[64,2048]{1,0:T(8,128)(4,1)S(1)} %copy-done.32), kind=kOutput, calls=%fused_computation.35 | convolution fusion | flops 139984896 | bytes 5439744 | tf_op jit(solution)/shard_map/qhd,khd->hqk/dot_general | solution.py:441
  109.6 0.8 fusion.19
  110.6 1.0 fusion.70
  111.5 1.6 %fusion.68 = f32[64,512]{1,0:T(8,128)} fusion(bf16[64,512]{1,0:T(8,128)(2,1)S(1)} %fusion.33, bf16[64,1024]{1,0:T(8,128)(2,1)} %copy-done.23, s32[]{:T(128)S(6)} %select_n.40), kind=kOutput, calls=%fused_computation.118 | convolution fusion | flops 4194304 | bytes 212996 | tf_op jit(solution)/shard_map/dot_general | solution.py:456
  113.2 1.6 %stack_reshape.14 = f32[64,4,1,128]{3,1,0,2:T(4,128)} reshape(f32[64,512]{1,0:T(8,128)} %fusion.68) | data formatting | bytes 262144 | tf_op jit(solution)/shard_map/stack;reshape | solution.py:460
  116.3 1.4 %copy-done.8 = f32[2048,512]{0,1:T(8,128)S(1)} copy-done((f32[2048,512]{0,1:T(8,128)S(1)}, f32[2048,512]{0,1:T(8,128)}, u32[]{:S(2)}) %copy-start.8) | copy-done | bytes 4194328
  117.7 1.5 %fusion.14 = bf16[2048,512]{0,1:T(8,128)(2,1)S(1)} fusion(f32[4,128,2048]{2,1,0:T(8,128)S(1)} %convolution_multiply_fusion, f32[2048,512]{0,1:T(8,128)S(1)} %copy-done.8), kind=kLoop, calls=%fused_computation.21 | loop fusion | flops 9437184 | bytes 10485760 | tf_op jit(solution)/shard_map/convert_element_type | solution.py:447
  119.2 1.1 fusion.37
  120.4 2.1 %fusion.24 = f32[64,512]{1,0:T(8,128)S(1)} fusion(bf16[2048,512]{0,1:T(8,128)(2,1)S(1)} %fusion.14, bf16[2048,1024]{1,0:T(8,128)(2,1)} %copy-done.4, s32[]{:T(128)S(6)} %select_n.40), kind=kOutput, calls=%fused_computation.59 | convolution fusion | flops 134217728 | bytes 2752516 | tf_op jit(solution)/shard_map/dot_general | solution.py:456
  123.9 1.4 %copy-done.7 = f32[2048,512]{0,1:T(8,128)S(1)} copy-done((f32[2048,512]{0,1:T(8,128)S(1)}, f32[2048,512]{0,1:T(8,128)}, u32[]{:S(2)}) %copy-start.7) | copy-done | bytes 4194328
  125.4 1.5 %fusion.13 = bf16[2048,512]{0,1:T(8,128)(2,1)S(1)} fusion(f32[4,128,2048]{2,1,0:T(8,128)S(1)} %fusion.94, f32[2048,512]{0,1:T(8,128)S(1)} %copy-done.7), kind=kLoop, calls=%fused_computation.19 | loop fusion | flops 9437184 | bytes 10485760 | tf_op jit(solution)/shard_map/convert_element_type | solution.py:448
  126.9 2.2 %fusion.26 = f32[64,512]{1,0:T(8,128)S(1)} fusion(bf16[2048,512]{0,1:T(8,128)(2,1)S(1)} %fusion.13, bf16[2048,1024]{1,0:T(8,128)(2,1)} %copy-done.4, s32[]{:T(128)S(6)} %select_n.40), kind=kOutput, calls=%fused_computation.61 | convolution fusion | flops 134217728 | bytes 2752516 | tf_op jit(solution)/shard_map/dot_general | solution.py:456
  129.2 1.1 convolution_add_fusion.2
  130.3 2.3 %convolution_add_fusion.1 = f32[128,1024]{1,0:T(8,128)} fusion(f32[128,1024]{1,0:T(8,128)} %convolution_add_fusion.2, bf16[1024,512]{0,1:T(8,128)(2,1)S(1)} %bitcast.136, bf16[64,512]{1,0:T(8,128)(2,1)S(1)} %fusion.33, s32[64]{0:T(128)S(1)} %copy-done.35, s32[128]{0:T(128)S(1)} %copy-done.36), kind=kOutput, calls=%fused_computation.39 | convolution fusion | flops 142811136 | bytes 2163456 | tf_op jit(solution)/shard_map/dot_general | solution.py:479
  132.7 1.6 %convolution_add_fusion.part = f32[128,1024]{1,0:T(8,128)S(1)} fusion(f32[128,1024]{1,0:T(8,128)} %convolution_add_fusion.1, bf16[1024,512]{0,1:T(8,128)(2,1)S(1)} %bitcast.134, bf16[64,512]{1,0:T(8,128)(2,1)S(1)} %fusion.32, s32[64]{0:T(128)S(1)} %copy-done.35, s32[128]{0:T(128)S(1)} %copy-done.36), kind=kOutput, calls=%fused_computation.38 | convolution fusion | flops 142811136 | bytes 2163456 | tf_op jit(solution)/shard_map/dot_general | solution.py:479
  134.2 2.0 %core_sum.1 = f32[128,1024]{1,0:T(8,128)S(1)} custom-call(f32[128,1024]{1,0:T(8,128)S(1)} %convolution_add_fusion.part), custom_call_target="tpu_custom_call" | custom-call | tf_op jit(solution)/shard_map/core_sum/pallas_call | solution.py:329
  136.3 1.2 fusion.86
  138.0 1.0 reshape.151
  139.0 1.0 convolution_add_fusion.3
  (119 shorter events, 12.2 us)
Async XLA Ops:
  0.6 6.0 %copy-start = (bf16[512,1024]{1,0:T(8,128)(2,1)S(1)}, bf16[512,1024]{1,0:T(8,128)(2,1)}, u32[]{:S(2)}) copy-start(bf16[512,1024]{1,0:T(8,128)(2,1)} %param.14) | copy-start | bytes 3145732
  6.7 58.1 %copy-start.31 = (pred[64,2048]{1,0:T(8,128)(4,1)}, pred[64,2048]{1,0:T(8,128)(4,1)S(1)}, u32[]{:S(2)}) copy-start(pred[64,2048]{1,0:T(8,128)(4,1)S(1)} %iota_compare_fusion.1) | copy-start | bytes 393220
  16.0 2.9 %copy-start.2 = (bf16[512,512]{1,0:T(8,128)(2,1)S(1)}, bf16[512,512]{1,0:T(8,128)(2,1)}, u32[]{:S(2)}) copy-start(bf16[512,512]{1,0:T(8,128)(2,1)} %user.1) | copy-start | bytes 1572868
  16.0 2.9 %copy-start.3 = (bf16[128,512]{1,0:T(8,128)(2,1)S(1)}, bf16[128,512]{1,0:T(8,128)(2,1)}, u32[]{:S(2)}) copy-start(bf16[128,512]{1,0:T(8,128)(2,1)} %history.1) | copy-start | bytes 393220
  18.9 40.7 %copy-start.5 = (bf16[1024,4,1,128]{0,3,2,1:T(8,128)(2,1)}, bf16[1024,4,1,128]{0,3,2,1:T(8,128)(2,1)S(1)}, u32[]{:S(2)}) copy-start(bf16[1024,4,1,128]{0,3,2,1:T(8,128)(2,1)S(1)} %get-tuple-element.15) | copy-start | bytes 3145732
  18.9 41.1 %copy-start.14 = (bf16[1024,4,1,128]{0,3,2,1:T(8,128)(2,1)}, bf16[1024,4,1,128]{0,3,2,1:T(8,128)(2,1)S(1)}, u32[]{:S(2)}) copy-start(bf16[1024,4,1,128]{0,3,2,1:T(8,128)(2,1)S(1)} %get-tuple-element.17) | copy-start | bytes 3145732
  18.9 48.3 %copy-start.12 = (bf16[1024,4,1,128]{0,3,2,1:T(8,128)(2,1)}, bf16[1024,4,1,128]{0,3,2,1:T(8,128)(2,1)S(1)}, u32[]{:S(2)}) copy-start(bf16[1024,4,1,128]{0,3,2,1:T(8,128)(2,1)S(1)} %get-tuple-element.18) | copy-start | bytes 3145732
  52.2 4.8 %copy-start.1 = (bf16[2048,1024]{1,0:T(8,128)(2,1)}, bf16[2048,1024]{1,0:T(8,128)(2,1)S(1)}, u32[]{:S(2)}) copy-start(bf16[2048,1024]{1,0:T(8,128)(2,1)S(1)} %get-tuple-element.6) | copy-start | bytes 12582916
  52.4 3.1 %copy-start.38 = (f32[128]{0:T(128)}, f32[128]{0:T(128)S(1)}, u32[]{:S(2)}) copy-start(f32[128]{0:T(128)S(1)} %broadcast_multiply_fusion.7) | copy-start | bytes 1540
  53.4 2.1 %copy-start.35 = (s32[64]{0:T(128)S(1)}, s32[64]{0:T(128)}, u32[]{:S(2)}) copy-start(s32[64]{0:T(128)} %param.18) | copy-start | bytes 772
  58.2 9.1 %copy-start.4 = (bf16[2048,1024]{1,0:T(8,128)(2,1)}, bf16[2048,1024]{1,0:T(8,128)(2,1)S(1)}, u32[]{:S(2)}) copy-start(bf16[2048,1024]{1,0:T(8,128)(2,1)S(1)} %fusion.3) | copy-start | bytes 12582916
  59.1 5.6 %copy-start.23 = (bf16[64,1024]{1,0:T(8,128)(2,1)}, bf16[64,1024]{1,0:T(8,128)(2,1)S(1)}, u32[]{:S(2)}) copy-start(bf16[64,1024]{1,0:T(8,128)(2,1)S(1)} %convolution_convert_fusion) | copy-start | bytes 393220
  60.0 4.7 %copy-start.24 = (f32[64,512]{1,0:T(8,128)}, f32[64,512]{1,0:T(8,128)S(1)}, u32[]{:S(2)}) copy-start(f32[64,512]{1,0:T(8,128)S(1)} %fusion.90) | copy-start | bytes 393220
  60.0 4.7 %copy-start.41 = (f32[64]{0:T(128)S(1)}, f32[64]{0:T(128)}, u32[]{:S(2)}) copy-start(f32[64]{0:T(128)} %add_convert_fusion.2) | copy-start | bytes 772
  64.7 2.5 %copy-start.17 = (bf16[2048,512]{0,1:T(8,128)(2,1)}, bf16[2048,512]{0,1:T(8,128)(2,1)S(1)}, u32[]{:S(2)}) copy-start(bf16[2048,512]{0,1:T(8,128)(2,1)S(1)} %get-tuple-element.25) | copy-start | bytes 6291460
  67.2 4.7 %copy-start.10 = (bf16[4,64,2048]{2,1,0:T(8,128)(2,1)}, bf16[4,64,2048]{2,1,0:T(8,128)(2,1)S(1)}, u32[]{:S(2)}) copy-start(bf16[4,64,2048]{2,1,0:T(8,128)(2,1)S(1)} %get-tuple-element.27) | copy-start | bytes 3145732
  67.3 6.4 %copy-start.9 = (bf16[512,1024]{1,0:T(8,128)(2,1)S(1)}, bf16[512,1024]{1,0:T(8,128)(2,1)}, u32[]{:S(2)}) copy-start(bf16[512,1024]{1,0:T(8,128)(2,1)} %param.13) | copy-start | bytes 3145732
  72.0 1.3 copy-start.19
  72.0 6.5 %copy-start.40 = (f32[512]{0:T(512)S(1)}, f32[512]{0:T(512)}, u32[]{:S(2)}) copy-start(f32[512]{0:T(512)} %param.17) | copy-start | bytes 6148
  72.0 9.2 %copy-start.34 = (s32[4,512]{1,0:T(4,128)S(1)}, s32[4,512]{1,0:T(4,128)}, u32[]{:S(2)}) copy-start(s32[4,512]{1,0:T(4,128)} %param.20) | copy-start | bytes 24580
  72.0 13.1 %copy-start.33 = (s32[4,512]{1,0:T(4,128)S(1)}, s32[4,512]{1,0:T(4,128)}, u32[]{:S(2)}) copy-start(s32[4,512]{1,0:T(4,128)} %param.21) | copy-start | bytes 24580
  101.1 6.3 %copy-start.20 = (bf16[2048,512]{0,1:T(8,128)(2,1)S(1)}, bf16[2048,512]{0,1:T(8,128)(2,1)}, u32[]{:S(2)}) copy-start(bf16[2048,512]{0,1:T(8,128)(2,1)} %copy-done.19) | copy-start | bytes 6291460
  101.1 6.3 %copy-start.32 = (pred[64,2048]{1,0:T(8,128)(4,1)S(1)}, pred[64,2048]{1,0:T(8,128)(4,1)}, u32[]{:S(2)}) copy-start(pred[64,2048]{1,0:T(8,128)(4,1)} %copy-done.31) | copy-start | bytes 393220
  101.1 6.3 %copy-start.42 = (f32[4,64,2048]{2,1,0:T(8,128)S(1)}, f32[4,64,2048]{2,1,0:T(8,128)}, u32[]{:S(2)}) copy-start(f32[4,64,2048]{2,1,0:T(8,128)} %get-tuple-element.28) | copy-start | bytes 6291460
  103.5 3.9 %copy-start.21 = (f32[64,1024]{1,0:T(8,128)}, f32[64,1024]{1,0:T(8,128)S(1)}, u32[]{:S(2)}) copy-start(f32[64,1024]{1,0:T(8,128)S(1)} %fusion.93) | copy-start | bytes 786436
  106.4 1.0 copy-start.29
  107.4 2.1 %copy-start.18 = (bf16[2048,512]{0,1:T(8,128)(2,1)S(1)}, bf16[2048,512]{0,1:T(8,128)(2,1)}, u32[]{:S(2)}) copy-start(bf16[2048,512]{0,1:T(8,128)(2,1)} %copy-done.17) | copy-start | bytes 6291460
  107.4 3.0 %copy-start.25 = (f32[64,512]{1,0:T(8,128)S(1)}, f32[64,512]{1,0:T(8,128)}, u32[]{:S(2)}) copy-start(f32[64,512]{1,0:T(8,128)} %copy-done.24) | copy-start | bytes 393220
  115.5 2.2 %copy-start.8 = (f32[2048,512]{0,1:T(8,128)S(1)}, f32[2048,512]{0,1:T(8,128)}, u32[]{:S(2)}) copy-start(f32[2048,512]{0,1:T(8,128)} %get-tuple-element.26) | copy-start | bytes 12582916
  117.7 1.5 %copy-start.15 = (bf16[1024,4,1,128]{0,3,2,1:T(8,128)(2,1)S(1)}, bf16[1024,4,1,128]{0,3,2,1:T(8,128)(2,1)}, u32[]{:S(2)}) copy-start(bf16[1024,4,1,128]{0,3,2,1:T(8,128)(2,1)} %copy-done.14) | copy-start | bytes 3145732
  119.2 4.0 %copy-start.11 = (bf16[4,64,2048]{2,1,0:T(8,128)(2,1)S(1)}, bf16[4,64,2048]{2,1,0:T(8,128)(2,1)}, u32[]{:S(2)}) copy-start(bf16[4,64,2048]{2,1,0:T(8,128)(2,1)} %copy-done.10) | copy-start | bytes 3145732
  119.2 4.0 %copy-start.30 = (bf16[64,4,128]{2,0,1:T(8,128)(2,1)S(1)}, bf16[64,4,128]{2,0,1:T(8,128)(2,1)}, u32[]{:S(2)}) copy-start(bf16[64,4,128]{2,0,1:T(8,128)(2,1)} %copy-done.29) | copy-start | bytes 196612
  123.2 2.2 %copy-start.7 = (f32[2048,512]{0,1:T(8,128)S(1)}, f32[2048,512]{0,1:T(8,128)}, u32[]{:S(2)}) copy-start(f32[2048,512]{0,1:T(8,128)} %get-tuple-element.24) | copy-start | bytes 12582916
  125.4 3.8 %copy-start.13 = (bf16[1024,4,1,128]{0,3,2,1:T(8,128)(2,1)S(1)}, bf16[1024,4,1,128]{0,3,2,1:T(8,128)(2,1)}, u32[]{:S(2)}) copy-start(bf16[1024,4,1,128]{0,3,2,1:T(8,128)(2,1)} %copy-done.12) | copy-start | bytes 3145732
  125.4 3.8 %copy-start.16 = (f32[128,1024]{1,0:T(8,128)S(1)}, f32[128,1024]{1,0:T(8,128)}, u32[]{:S(2)}) copy-start(f32[128,1024]{1,0:T(8,128)} %fusion.37) | copy-start | bytes 1572868
  126.9 3.4 %copy-start.6 = (bf16[1024,4,1,128]{0,3,2,1:T(8,128)(2,1)S(1)}, bf16[1024,4,1,128]{0,3,2,1:T(8,128)(2,1)}, u32[]{:S(2)}) copy-start(bf16[1024,4,1,128]{0,3,2,1:T(8,128)(2,1)} %copy-done.5) | copy-start | bytes 3145732
  126.9 3.4 %copy-start.36 = (s32[128]{0:T(128)S(1)}, s32[128]{0:T(128)}, u32[]{:S(2)}) copy-start(s32[128]{0:T(128)} %iota_add_fusion) | copy-start | bytes 1540
  129.2 7.1 %copy-start.37 = (f32[128]{0:T(128)S(1)}, f32[128]{0:T(128)}, u32[]{:S(2)}) copy-start(f32[128]{0:T(128)} %add_rsqrt_fusion.2) | copy-start | bytes 1540
  129.2 7.1 %copy-start.39 = (f32[128]{0:T(128)S(1)}, f32[128]{0:T(128)}, u32[]{:S(2)}) copy-start(f32[128]{0:T(128)} %copy-done.38) | copy-start | bytes 1540
  129.2 8.3 %copy-start.26 = (f32[64,4,1,128]{3,1,0,2:T(4,128)S(1)}, f32[64,4,1,128]{3,1,0,2:T(4,128)}, u32[]{:S(2)}) copy-start(f32[64,4,1,128]{3,1,0,2:T(4,128)} %stack_reshape.14) | copy-start | bytes 393220
  132.7 4.9 %copy-start.27 = (f32[64,4,1,128]{3,1,0,2:T(4,128)S(1)}, f32[64,4,1,128]{3,1,0,2:T(4,128)}, u32[]{:S(2)}) copy-start(f32[64,4,1,128]{3,1,0,2:T(4,128)} %stack_reshape.12) | copy-start | bytes 393220
  132.7 4.9 %copy-start.28 = (f32[64,4,1,128]{3,1,0,2:T(4,128)S(1)}, f32[64,4,1,128]{3,1,0,2:T(4,128)}, u32[]{:S(2)}) copy-start(f32[64,4,1,128]{3,1,0,2:T(4,128)} %stack_reshape.15) | copy-start | bytes 393220
  132.7 6.4 %copy-start.22 = (f32[64,1024]{1,0:T(8,128)S(1)}, f32[64,1024]{1,0:T(8,128)}, u32[]{:S(2)}) copy-start(f32[64,1024]{1,0:T(8,128)} %copy-done.21) | copy-start | bytes 786436

commit v3 on v2

--- a/solution.py
+++ b/solution.py
@@ -37,6 +37,10 @@
     return jnp.dot(left, right, preferred_element_type=F32)
 
 
+def back(grads, weights):
+    return lax.dot_general(grads, weights, (((1,), (1,)), ((), ())), preferred_element_type=F32)
+
+
 MESH = pl.DeviceIdType.MESH
 VMEM = pl.BlockSpec(memory_space=pltpu.VMEM)
 DMA = pltpu.SemaphoreType.DMA
@@ -44,7 +48,7 @@
 
 def kernel_params(collective_id):
     return pltpu.CompilerParams(
-        collective_id=collective_id, has_side_effects=True, vmem_limit_bytes=48 * 1024 * 1024
+        collective_id=collective_id, has_side_effects=True, vmem_limit_bytes=60 * 1024 * 1024
     )
 
 
@@ -68,10 +72,35 @@
 def history_kernel(
     ctx_count,
     cand_count,
+    heads,
     history,
     user,
+    points,
+    head_weights,
+    cand_table,
+    item_weights,
+    x_low,
+    before_key,
+    before_value,
+    key_heads,
+    values,
+    x_requests,
+    raw_requests,
+    before_query,
+    before_gate,
+    attended,
+    x_own,
+    x_inverse,
+    user_full,
+    item_proj,
     features,
-    user_full,
+    weights,
+    table,
+    item,
+    x_sum,
+    raw_sum,
+    weight_sem,
+    item_sem,
     line_send,
     first_send,
     second_send,
@@ -150,12 +179,69 @@
         )
         copy.start()
         pending.append(copy)
+    weight_copies = []
+    for head in range(heads):
+        for section in range(4):
+            copy = pltpu.make_async_copy(
+                head_weights.at[:, pl.ds((4 * head + section) * HEAD, HEAD)],
+                weights.at[section, :, pl.ds(head * HEAD, HEAD)],
+                weight_sem.at[4 * head + section],
+            )
+            copy.start()
+            weight_copies.append(copy)
+    item_copies = [
+        pltpu.make_async_copy(cand_table, table, item_sem.at[0]),
+        pltpu.make_async_copy(item_weights, item, item_sem.at[1]),
+    ]
+    for copy in item_copies:
+        copy.start()
     user_full[own_user, :] = user[...]
     features[pl.ds(pl.multiple_of(ctx * rows, rows), rows), columns] = history[...]
 
+    x_sum[...] = jnp.zeros_like(x_sum)
+    raw_sum[...] = jnp.zeros_like(raw_sum)
+    requests = points.shape[0]
+
+    def project(block):
+        for step in range(1, cand_count):
+            source = (cand + cand_count - step) % cand_count
+            there = pl.ds(pl.multiple_of(source * slice_width, slice_width), slice_width)
+            landed = features.at[pl.ds(pl.multiple_of(block * rows, rows), rows), there]
+            pltpu.make_async_remote_copy(
+                src_ref=landed,
+                dst_ref=landed,
+                send_sem=cand_send.at[0, 0],
+                recv_sem=cand_recv.at[block, step - 1],
+                device_id=(ctx, cand),
+                device_id_type=MESH,
+            ).wait_recv()
+        span = pl.ds(pl.multiple_of(block * rows, rows), rows)
+        raw = features[span, :]
+        normed, inverse = layer_norm(raw.astype(F32))
+        low_block = normed.astype(BF16)
+        x_low[span, :] = low_block
+        position = block * rows + lax.broadcasted_iota(jnp.int32, (requests, rows), 1)
+        picks = jnp.where(points[...] == position, 1.0, 0.0).astype(BF16)
+        x_sum[...] += mm(picks, low_block)
+        raw_sum[...] += mm(picks, raw)
+        key_part = mm(low_block, weights[3])
+        before_key[span, :] = key_part
+        key_heads[span, :] = (key_part * jax.nn.sigmoid(key_part)).astype(BF16)
+        value_part = mm(low_block, weights[1])
+        before_value[span, :] = value_part
+        values[span, :] = (value_part * jax.nn.sigmoid(value_part)).astype(BF16)
+        return normed, inverse
+
+    for copy in item_copies:
+        copy.wait()
+    item_proj[...] = mm(table[...], item[...])
+    for copy in weight_copies:
+        copy.wait()
+
     for step in range(depth):
+        line_block = flip(line, step) * 4 + low
         if step > 0:
-            block = flip(line, step) * 4 + low
+            block = line_block
             arrive(block)
             send(place(block), block, first_send.at[step], ctx_recv.at[block], (first, cand))
             send(place(block), block, second_send.at[step], ctx_recv.at[block], (second, cand))
@@ -164,25 +250,50 @@
         arrive(block)
         send(place(block), block, second_send.at[depth + step], ctx_recv.at[block], (second, cand))
         share(place(block), block, depth + step)
+        normed, inverse = project(line_block)
+        if step == 0:
+            x_own[...] = normed
+            x_inverse[...] = inverse
     for step in range(depth):
+        lines = flip(line, step) * 4
         for part, corner in enumerate((second % 4, 3 - low)):
-            block = flip(line, step) * 4 + corner
+            block = lines + corner
             arrive(block)
             share(place(block), block, (2 + part) * depth + step)
+            project(lines + (first % 4, second % 4)[part])
+        if step > 0:
+            project(flip(line, step - 1) * 4 + 3 - low)
+    project(flip(line, depth - 1) * 4 + 3 - low)
+
+    x_request = x_sum[...].astype(BF16)
+    x_requests[...] = x_request
+    raw_requests[...] = raw_sum[...]
+    query_part = mm(x_request, weights[2])
+    before_query[...] = query_part
+    before_gate[...] = mm(x_request, weights[0])
+    queries = (query_part * jax.nn.sigmoid(query_part)).astype(BF16)
+    divisor = (points[...] + 1).astype(F32)
+    chunk = 4 * rows
+    for head in range(heads):
+        span = pl.ds(head * HEAD, HEAD)
+        query = queries[:, head * HEAD : (head + 1) * HEAD]
+
+        def add_chunk(index, total):
+            start = pl.multiple_of(index * chunk, chunk)
+            logits = back(query, key_heads[pl.ds(start, chunk), span]) * HEAD ** (-0.5)
+            position = start + lax.broadcasted_iota(jnp.int32, (requests, chunk), 1)
+            weight = jnp.where(
+                position <= points[...], logits * jax.nn.sigmoid(logits) / divisor, 0.0
+            ).astype(BF16)
+            return total + mm(weight, values[pl.ds(start, chunk), span])
+
+        attended[:, span] = lax.fori_loop(
+            0, ctx_count * rows // chunk, add_chunk, jnp.zeros((requests, HEAD), F32)
+        )
+
     for step in range(1, cand_count):
         source = (cand + cand_count - step) % cand_count
-        there = pl.ds(pl.multiple_of(source * slice_width, slice_width), slice_width)
         user_there = pl.ds(pl.multiple_of(source * user_rows, user_rows), user_rows)
-        for block in range(ctx_count):
-            landed = features.at[pl.ds(block * rows, rows), there]
-            pltpu.make_async_remote_copy(
-                src_ref=landed,
-                dst_ref=landed,
-                send_sem=cand_send.at[0, 0],
-                recv_sem=cand_recv.at[block, step - 1],
-                device_id=(ctx, cand),
-                device_id_type=MESH,
-            ).wait_recv()
         pltpu.make_async_remote_copy(
             src_ref=user_full.at[user_there],
             dst_ref=user_full.at[user_there],
@@ -195,21 +306,49 @@
         copy.wait_send()
 
 
-def gather_history(history, user_weights):
+def gather_history(history, user_weights, points, head_weights, cand_table, item_weights):
     ctx_count, cand_count = lax.axis_size("ctx"), lax.axis_size("cand")
     rows, slice_width = history.shape
     user_rows, hidden = user_weights.shape
+    requests = points.shape[0]
+    width = head_weights.shape[0]
+    length = rows * ctx_count
+    cols = head_weights.shape[1] // 4
+    heads = cols // HEAD
     depth = ctx_count // 4
     others = cand_count - 1
+    shape = jax.ShapeDtypeStruct
+    outputs = (
+        shape((length, width), BF16),
+        shape((length, cols), F32),
+        shape((length, cols), F32),
+        shape((length, cols), BF16),
+        shape((length, cols), BF16),
+        shape((requests, width), BF16),
+        shape((requests, width), F32),
+        shape((requests, cols), F32),
+        shape((requests, cols), F32),
+        shape((requests, cols), F32),
+        shape((rows, width), F32),
+        shape((rows, 1), F32),
+        shape((user_rows * cand_count, hidden), BF16),
+        shape((cand_table.shape[0], hidden), F32),
+    )
+    anywhere = pl.BlockSpec(memory_space=pl.ANY)
     return pl.pallas_call(
-        functools.partial(history_kernel, ctx_count, cand_count),
-        out_shape=(
-            jax.ShapeDtypeStruct((rows * ctx_count, slice_width * cand_count), history.dtype),
-            jax.ShapeDtypeStruct((user_rows * cand_count, hidden), user_weights.dtype),
-        ),
-        in_specs=[VMEM, VMEM],
-        out_specs=(VMEM, VMEM),
+        functools.partial(history_kernel, ctx_count, cand_count, heads),
+        out_shape=outputs,
+        in_specs=[VMEM] * 3 + [anywhere] * 3,
+        out_specs=(VMEM,) * len(outputs),
         scratch_shapes=[
+            pltpu.VMEM((length, width), BF16),
+            pltpu.VMEM((4, width, cols), BF16),
+            pltpu.VMEM(cand_table.shape, BF16),
+            pltpu.VMEM(item_weights.shape, BF16),
+            pltpu.VMEM((requests, width), F32),
+            pltpu.VMEM((requests, width), F32),
+            DMA((4 * heads,)),
+            DMA((2,)),
             DMA((max(depth - 1, 1),)),
             DMA((depth,)),
             DMA((2 * depth,)),
@@ -220,8 +359,8 @@
             DMA((others,)),
         ],
         compiler_params=kernel_params(0),
-        name="history_gather",
-    )(history, user_weights)
+        name="history_project",
+    )(history, user_weights, points, head_weights, cand_table, item_weights)
 
 
 def swap_cores(cand_count, source, slots, send_sem, recv_sem):
@@ -370,25 +509,31 @@
     gate_w, value_w, query_w, key_w = (
         sections[:, :, index].reshape(width, cols) for index in range(4)
     )
-    item_proj = mm(cand_table, item_weights)
-    features, user_full = gather_history(history, user_weights)
-    length = features.shape[0]
-    x_low = layer_norm(features.astype(F32))[0].astype(BF16)
-
-    picks = (request_points[:, None] == jnp.arange(length, dtype=jnp.int32)[None, :]).astype(BF16)
-    x_requests = mm(picks, x_low).astype(BF16)
-    raw_requests = mm(picks, features)
-
-    before_key = mm(x_low, key_w)
-    before_value = mm(x_low, value_w)
-    before_query = mm(x_requests, query_w)
-    before_gate = mm(x_requests, gate_w)
+    (
+        x_low,
+        before_key,
+        before_value,
+        key_heads,
+        values,
+        x_requests,
+        raw_requests,
+        before_query,
+        before_gate,
+        attended,
+        x_normed,
+        x_inverse,
+        user_full,
+        item_proj,
+    ) = gather_history(
+        history, user_weights, request_points[:, None], head_weights, cand_table, item_weights
+    )
+    length = x_low.shape[0]
 
     def split(array):
         return array.reshape(array.shape[0], heads, HEAD)
 
-    key_heads = split(jax.nn.silu(before_key).astype(BF16))
-    values = split(jax.nn.silu(before_value).astype(BF16))
+    key_heads = split(key_heads)
+    values = split(values)
     queries = split(jax.nn.silu(before_query).astype(BF16))
     gate_part = split(jax.nn.silu(before_gate).astype(BF16)).astype(F32)
 
@@ -396,8 +541,7 @@
     allowed = (jnp.arange(length, dtype=jnp.int32)[None, :] <= request_points[:, None])[None]
     divisor = (request_points + 1).astype(F32)[None, :, None]
     weight = jnp.where(allowed, jax.nn.silu(logits) / divisor, 0.0).astype(BF16)
-    attended = jnp.einsum("hqk,khd->qhd", weight, values, preferred_element_type=F32)
-    normed, inverse = layer_norm(attended)
+    normed, inverse = layer_norm(split(attended))
     gated = (normed * gate_part).astype(BF16).reshape(requests, cols)
 
     def own(array):
@@ -473,11 +617,6 @@
     positions = first_row + jnp.arange(row_count, dtype=jnp.int32)
     places = positions[:, None] == request_points[None, :]
     low_places = places.astype(BF16)
-    transposed = (((1,), (1,)), ((), ()))
-
-    def back(grads, weights):
-        return lax.dot_general(grads, weights, transposed, preferred_element_type=F32)
-
     d_normed = core_sum(
         back(own_rows(d_before_key), key_w)
         + back(own_rows(d_before_value), value_w)
@@ -485,7 +624,6 @@
         + back(mm(low_places, d_before_gate).astype(BF16), gate_w),
         2,
     )
-    x_normed, x_inverse = layer_norm(own_rows(features).astype(F32))
     column_start = cand_index * slice_width
     d_input = lax.dynamic_slice_in_dim(
         norm_back(d_normed, x_normed, x_inverse), column_start, slice_width, 1

time: 141 us -> 164 us (1.16)
  Pallas kernels: 43.8 us -> 70.6 us
  local copies, waits for them, and re-layouts: 17.7 us -> 28.1 us
  matrix products: 44.8 us -> 35.3 us
  other arithmetic: 26.3 us -> 21.9 us
    pallas_call x1, Pallas kernels: 33.3 us -> 56.6 us  [gather_history(): pl.pallas_call(functools.partial(history_kernel, ctx_count, cand_count, h...]
    dot_general x9 -> x2, matrix products: 17 us -> 1.73 us  [mm(): return jnp.dot(left, right, preferred_element_type=F32)]
    reshape x0 -> x3, local copies, waits for them, and re-layouts: none -> 11.7 us  [the longest x1 5.37 us: per_device(): d_key.reshape(length, cols) * silu_slope(before_key)]
    convert_element_type x1, other arithmetic: 1.51 us -> 8.34 us  [per_device(): (d_value.reshape(length, cols) * silu_slope(before_value)).astype(BF16)]
    unnamed x87 -> x43, local copies, waits for them, and re-layouts: 9.81 us -> 6.51 us
    dot_general x1, matrix products: 0.75 us -> 3.78 us  [per_device(): jnp.einsum('hqk,qhd->khd', weight, d_attended, preferred_element_type=F32)]
    dot_general x1, matrix products: 0.76 us -> 2.69 us  [per_device(): jnp.einsum('hqk,qhd->khd', d_logit, queries, preferred_element_type=F32)]
    pallas_call x1, Pallas kernels: 2 us -> 3.81 us  [core_sum(): pl.pallas_call(functools.partial(core_sum_kernel, cand_count), out_shape=...]
where the time goes in v3:
time: 164 us; the launch traced here: 163 us
  Pallas kernels  70.6 us (43%)
  matrix products  35.3 us (22%)
  local copies, waits for them, and re-layouts  28.1 us (17%)
  other arithmetic  21.9 us (13%)
  blocking collectives  6.03 us (4%)
    pallas_call x1, Pallas kernels, gather_history(): pl.pallas_call(functools.partial(history_kernel, ctx_count, cand_count, h...  56.6 us
    pallas_call x1, Pallas kernels, gather_user_grad(): pl.pallas_call(functools.partial(user_grad_kernel, ctx_count, cand_count)...  10.2 us
    convert_element_type x1, other arithmetic, per_device(): (d_value.reshape(length, cols) * silu_slope(before_value)).astype(BF16)  8.34 us
    dot_general x4, matrix products, grad_of(): lax.dot_general(rows, grads, (((0,), (0,)), ((), ())), preferred_element_...  6.95 us
    dot_general x4, matrix products, back(): lax.dot_general(grads, weights, (((1,), (1,)), ((), ())), preferred_eleme...  6.76 us
    unnamed x43, local copies, waits for them, and re-layouts  6.51 us
    reshape x1, local copies, waits for them, and re-layouts, per_device(): d_key.reshape(length, cols) * silu_slope(before_key)  5.37 us
    reshape x1, local copies, waits for them, and re-layouts, per_device(): d_value.reshape(length, cols) * silu_slope(before_value)  5.35 us

profile of v3, /device:TPU:0, one launch (start us, length us, event | category | flops | bytes accessed | tf_op | source)
XLA Modules:
  0.0 163.1 jit_solution(2445024725928540431)
XLA Ops:
  0.6 1.4 copy.74.points
  2.1 56.6 %history_project.1 = (bf16[2048,1024]{1,0:T(8,128)(2,1)}, f32[2048,512]{1,0:T(8,128)}, f32[2048,512]{1,0:T(8,128)}, bf16[2048,512]{1,0:T(8,128)(2,1)}, bf16[2048...) custom-call(bf16[128,512]{1,0:T(8,128)(2,1)} %history.1, ...), custom_call_target="tpu_custom_call" | custom-call | tf_op jit(solution)/shard_map/history_project/pallas_call | solution.py:338
  58.7 1.0 reshape.117
  59.9 0.2 multiply_reduce_fusion.2
  60.4 1.0 fusion.37
  61.5 0.3 fusion.77
  61.7 3.5 %psum.14 = f32[4,1024]{1,0:T(4,128)S(1)} all-reduce(f32[4,1024]{1,0:T(4,128)S(1)} %fusion.77), channel_id=1, replica_groups=mesh['ctx'=16,'cand'=2] {'cand'}, use_global_device_ids=true, to_apply=%region_2.3 | all-reduce | flops 4096 | bytes 32768 | tf_op jit(solution)/shard_map/psum | solution.py:550
  65.2 1.5 fusion.76
  66.7 2.7 %fusion.4 = f32[4,512]{1,0:T(4,128)S(1)} fusion(f32[512]{0:T(512)S(1)} %copy-done.20, f32[512,512]{1,0:T(8,128)} %get-tuple-element.22, f32[4,512]{1,0:T(4,128)S(1)} %fusion.76), kind=kLoop, calls=%fused_computation.7 | loop fusion | flops 7337984 | bytes 1067008 | tf_op jit(solution)/shard_map/reduce_sum | solution.py:558
  69.4 1.4 select_reduce_fusion.1
  70.8 2.5 %psum.15 = f32[4,512]{1,0:T(4,128)S(1)} all-reduce(f32[4,512]{1,0:T(4,128)S(1)} %select_reduce_fusion.1), channel_id=1, replica_groups=mesh['ctx'=16,'cand'=2] {'cand'}, use_global_device_ids=true, to_apply=%region_5.6 | all-reduce | flops 2048 | bytes 16384 | tf_op jit(solution)/shard_map/psum | solution.py:559
  73.5 0.2 exponential_reduce_fusion
  73.7 0.5 fusion.94
  74.3 1.2 select_reduce_fusion
  75.4 2.8 %fusion.8 = f32[4,512]{1,0:T(4,128)S(1)} fusion(f32[4,512]{1,0:T(4,128)S(1)} %select_reduce_fusion, f32[512,512]{1,0:T(8,128)} %get-tuple-element.22, f32[4,512]{1,0:T(4,128)S(1)} %fusion.76), kind=kLoop, calls=%fused_computation.11 | loop fusion | flops 10483712 | bytes 1073152 | tf_op jit(solution)/shard_map/reduce_sum | solution.py:566
  78.2 0.6 broadcast_multiply_fusion.3.part
  78.8 10.2 %user_grad_gather.1 = f32[16,4,512]{2,1,0:T(4,128)} custom-call(f32[4,512]{1,0:T(4,128)} %broadcast_multiply_fusion.3.part), custom_call_target="tpu_custom_call" | custom-call | tf_op jit(solution)/shard_map/user_grad_gather/pallas_call | solution.py:438
  89.0 1.0 reshape.118
  90.2 0.3 fusion.68
  90.4 1.1 fusion.95
  91.5 1.7 %multiply_convert_fusion.2 = (bf16[64,512]{1,0:T(8,128)(2,1)}, f32[64,512]{1,0:T(8,128)S(1)}) fusion(f32[64,512]{1,0:T(8,128)S(1)} %copy-done.9, f32[8,8,4,128]{3,2,1,0:T(4,128)S(1)} %bitcast.97, f32[64,512]{1,0:T(8,128)S(1)} %copy-done.4, f32[8,8,4,128]{3,2,1,0:T(4,128)S(1)} %bitcast.99, f32[64,1024]{1,0:T(8,128)S(1)} %fusion.95, ...), kind=kOutput, calls=%fused_computation.64 | convolution fusion | flops 403177472 | bytes 2031616 | tf_op jit(solution)/shard_map/dot_general | solution.py:575
  93.3 0.4 fusion.92
  93.7 0.3 multiply_convert_fusion.3
  94.0 2.5 %convolution_multiply_fusion.1 = f32[4,64,2048]{2,1,0:T(8,128)S(1)} fusion(bf16[2048,512]{1,0:T(8,128)(2,1)} %get-tuple-element.26, f32[64,512]{1,0:T(8,128)S(1)} %copy-done.5), kind=kOutput, calls=%fused_computation.19 | convolution fusion | flops 134905856 | bytes 4325376 | tf_op jit(solution)/shard_map/qhd,khd->hqk/dot_general | solution.py:540
  96.7 2.9 %fusion.12 = bf16[4,64,2048]{2,1,0:T(8,128)(2,1)S(1)} fusion(f32[4,64,2048]{2,1,0:T(8,128)S(1)} %convolution_multiply_fusion.1, f32[64]{0:T(128)S(1)} %add_convert_fusion.2, pred[64,2048]{1,0:T(8,128)(4,1)S(1)} %iota_compare_fusion.1, bf16[64,4,128]{2,1,0:T(4,128)(2,1)S(1)} %multiply_convert_fusion.3, bf16[2048,512]{1,0:T(8,128)(2,1)} %get-tuple-element.25), kind=kOutput, calls=%fused_computation.23 | convolution fusion | flops 139984896 | bytes 5439744 | tf_op jit(solution)/shard_map/qhd,khd->hqk/dot_general | solution.py:585
  99.6 2.7 %convolution_multiply_fusion = f32[4,128,2048]{2,1,0:T(8,128)} fusion(bf16[4,64,2048]{2,1,0:T(8,128)(2,1)S(1)} %fusion.12, f32[64,512]{1,0:T(8,128)S(1)} %copy-done.5), kind=kOutput, calls=%fused_computation.18 | convolution fusion | flops 135430144 | bytes 5373952 | tf_op jit(solution)/shard_map/hqk,qhd->khd/dot_general | solution.py:588
  102.3 5.4 %copy.87 = f32[2048,512]{1,0:T(8,128)} copy(f32[2048,512]{0,1:T(8,128)} %bitcast.90) | data formatting | bytes 8388608 | tf_op jit(solution)/shard_map/reshape | solution.py:591
  107.6 3.8 %fusion.26 = f32[4,128,2048]{2,1,0:T(8,128)} fusion(f32[4,64,2048]{2,1,0:T(8,128)S(1)} %convolution_multiply_fusion.1, f32[64]{0:T(128)S(1)} %add_convert_fusion.2, pred[64,2048]{1,0:T(8,128)(4,1)} %copy-done.13, bf16[64,4,128]{2,1,0:T(4,128)(2,1)} %copy-done.15), kind=kOutput, calls=%fused_computation.41 | convolution fusion | flops 137887744 | bytes 6488320 | tf_op jit(solution)/shard_map/hqk,qhd->khd/dot_general | solution.py:589
  111.4 5.4 %copy.88 = f32[2048,512]{1,0:T(8,128)} copy(f32[2048,512]{0,1:T(8,128)} %bitcast.91) | data formatting | bytes 8388608 | tf_op jit(solution)/shard_map/reshape | solution.py:592
  116.8 8.3 %multiply_convert_fusion = (bf16[2048,512]{1,0:T(8,128)(2,1)S(1)}, bf16[2048,512]{1,0:T(8,128)(2,1)}) fusion(f32[2048,512]{1,0:T(8,128)} %copy.88, f32[2048,512]{1,0:T(8,128)} %get-tuple-element.28, f32[2048,512]{1,0:T(8,128)} %copy.87, f32[2048,512]{1,0:T(8,128)} %get-tuple-element.27), kind=kLoop, calls=%fused_computation.12 | loop fusion | flops 18874368 | bytes 20971520 | tf_op jit(solution)/shard_map/convert_element_type | solution.py:592
  125.1 2.4 %fusion.33 = f32[64,512]{1,0:T(8,128)} fusion(bf16[2048,512]{1,0:T(8,128)(2,1)S(1)} %get-tuple-element.46, bf16[2048,1024]{1,0:T(8,128)(2,1)} %get-tuple-element.31, s32[]{:T(128)S(6)} %select_n.39), kind=kOutput, calls=%fused_computation.51 | convolution fusion | flops 134217728 | bytes 2752516 | tf_op jit(solution)/shard_map/dot_general | solution.py:600
  127.5 1.6 stack_reshape.13
  129.1 2.0 %fusion.23 = f32[4,8,8,128]{3,2,1,0:T(8,128)S(1)} fusion(bf16[4,64,2048]{2,1,0:T(8,128)(2,1)S(1)} %fusion.12, bf16[2048,512]{1,0:T(8,128)(2,1)} %get-tuple-element.26), kind=kOutput, calls=%fused_computation.40 | convolution fusion | flops 134250496 | bytes 3276800 | tf_op jit(solution)/shard_map/hqk,khd->qhd/dot_general | solution.py:587
  131.2 1.0 fusion.72
  132.3 2.5 %fusion.31 = f32[64,512]{1,0:T(8,128)S(1)} fusion(bf16[2048,512]{1,0:T(8,128)(2,1)} %get-tuple-element.47, bf16[2048,1024]{1,0:T(8,128)(2,1)} %get-tuple-element.31, s32[]{:T(128)S(6)} %select_n.39), kind=kOutput, calls=%fused_computation.49 | convolution fusion | flops 134217728 | bytes 2752516 | tf_op jit(solution)/shard_map/dot_general | solution.py:600
  134.8 1.1 fusion.74
  136.1 0.3 copy.86
  136.5 1.0 reshape.126
  137.5 6.4 %copy.81 = bf16[1024,2048]{0,1:T(8,128)(2,1)} copy(bf16[1024,2048]{1,0:T(8,128)(2,1)} %head_weights.1) | data formatting | bytes 8388608 | tf_op args[1]
  143.9 4.1 %fusion.93 = (bf16[1024,4,1,128]{0,3,2,1:T(8,128)(2,1)}, bf16[1024,4,1,128]{0,3,2,1:T(8,128)(2,1)}, bf16[1024,4,1,128]{0,3,2,1:T(8,128)(2,1)S(1)}, bf16[1024,4,1,128]{0,3,2,1:T(8,128)(2,1)S(1)}) fusion(bf16[1024,4,4,128]{0,3,2,1:T(8,128)(2,1)} %bitcast.89), kind=kLoop, calls=%fused_computation.140 | loop fusion | bytes 8388608 | tf_op jit(solution)/shard_map/slice | solution.py:510
  148.0 1.2 fusion.40
  149.3 1.1 convolution_add_fusion.2
  150.4 1.9 %convolution_add_fusion.1 = f32[128,1024]{1,0:T(8,128)S(1)} fusion(f32[128,1024]{1,0:T(8,128)} %convolution_add_fusion.2, bf16[1024,512]{0,1:T(8,128)(2,1)} %bitcast.95, bf16[64,512]{1,0:T(8,128)(2,1)S(1)} %copy-done.8, s32[64]{0:T(128)S(1)} %copy-done.18, s32[128]{0:T(128)S(1)} %iota_add_fusion), kind=kOutput, calls=%fused_computation.34 | convolution fusion | flops 142811136 | bytes 2163456 | tf_op jit(solution)/shard_map/dot_general | solution.py:41
  152.3 2.5 %convolution_add_fusion.part = f32[128,1024]{1,0:T(8,128)} fusion(f32[128,1024]{1,0:T(8,128)S(1)} %convolution_add_fusion.1, bf16[1024,512]{0,1:T(8,128)(2,1)} %bitcast.94, bf16[64,512]{1,0:T(8,128)(2,1)S(1)} %copy-done.6, s32[64]{0:T(128)S(1)} %copy-done.18, s32[128]{0:T(128)S(1)} %iota_add_fusion), kind=kOutput, calls=%fused_computation.33 | convolution fusion | flops 142811136 | bytes 2163456 | tf_op jit(solution)/shard_map/dot_general | solution.py:41
  154.8 3.8 %core_sum.1 = f32[128,1024]{1,0:T(8,128)} custom-call(f32[128,1024]{1,0:T(8,128)} %convolution_add_fusion.part), custom_call_target="tpu_custom_call" | custom-call | tf_op jit(solution)/shard_map/core_sum/pallas_call | solution.py:468
  158.7 1.3 fusion.91
  160.2 2.0 %convolution_add_fusion.3 = f32[128,512]{1,0:T(8,128)} fusion(f32[128,1024]{1,0:T(8,128)S(1)} %copy-done.3, s32[]{:T(128)S(6)} %select_n.35, f32[128,1024]{1,0:T(8,128)} %core_sum.1, f32[128]{0:T(128)S(1)} %reduce, f32[128]{0:T(128)S(1)} %broadcast_multiply_fusion.4, f32[128]{0:T(128)S(1)} %broadcast_multiply_fusion.5, f32[64,1024]{1,0:T(8,128)S(1)} %fusion.95, ...), kind=kOutput, calls=%fused_computation.36 | convolution fusion | flops 50667520 | bytes 921088 | tf_op jit(solution)/shard_map/dot_general | solution.py:632
  162.1 1.0 fusion.55
  (66 shorter events, 1.5 us)
Async XLA Ops:
  0.6 60.8 %copy-start = (bf16[512,1024]{1,0:T(8,128)(2,1)S(1)}, bf16[512,1024]{1,0:T(8,128)(2,1)}, u32[]{:S(2)}) copy-start(bf16[512,1024]{1,0:T(8,128)(2,1)} %param.13) | copy-start | bytes 3145732
  2.1 64.6 %copy-start.20 = (f32[512]{0:T(512)S(1)}, f32[512]{0:T(512)}, u32[]{:S(2)}) copy-start(f32[512]{0:T(512)} %param.17) | copy-start | bytes 6148
  58.7 10.7 %copy-start.19 = (s32[4,512]{1,0:T(4,128)S(1)}, s32[4,512]{1,0:T(4,128)}, u32[]{:S(2)}) copy-start(s32[4,512]{1,0:T(4,128)} %param.19) | copy-start | bytes 24580
  58.7 10.7 %copy-start.17 = (s32[4,512]{1,0:T(4,128)S(1)}, s32[4,512]{1,0:T(4,128)}, u32[]{:S(2)}) copy-start(s32[4,512]{1,0:T(4,128)} %param.20) | copy-start | bytes 24580
  58.7 14.6 %copy-start.14 = (s32[4,512]{1,0:T(4,128)S(1)}, s32[4,512]{1,0:T(4,128)}, u32[]{:S(2)}) copy-start(s32[4,512]{1,0:T(4,128)} %param.21) | copy-start | bytes 24580
  58.7 31.2 %copy-start.18 = (s32[64]{0:T(128)S(1)}, s32[64]{0:T(128)}, u32[]{:S(2)}) copy-start(s32[64]{0:T(128)} %param.18) | copy-start | bytes 772
  59.7 30.7 %copy-start.2 = (bf16[1024,512]{1,0:T(8,128)(2,1)S(1)}, bf16[1024,512]{1,0:T(8,128)(2,1)}, u32[]{:S(2)}) copy-start(bf16[1024,512]{1,0:T(8,128)(2,1)} %get-tuple-element.21) | copy-start | bytes 3145732
  61.4 17.4 %copy-start.11 = (bf16[64,512]{1,0:T(8,128)(2,1)}, bf16[64,512]{1,0:T(8,128)(2,1)S(1)}, u32[]{:S(2)}) copy-start(bf16[64,512]{1,0:T(8,128)(2,1)S(1)} %fusion.37) | copy-start | bytes 196612
  61.4 30.1 %copy-start.4 = (f32[64,512]{1,0:T(8,128)S(1)}, f32[64,512]{1,0:T(8,128)}, u32[]{:S(2)}) copy-start(f32[64,512]{1,0:T(8,128)} %get-tuple-element.19) | copy-start | bytes 393220
  61.5 30.1 %copy-start.9 = (f32[64,512]{1,0:T(8,128)S(1)}, f32[64,512]{1,0:T(8,128)}, u32[]{:S(2)}) copy-start(f32[64,512]{1,0:T(8,128)} %get-tuple-element.20) | copy-start | bytes 393220
  69.4 24.6 %copy-start.5 = (f32[64,512]{1,0:T(8,128)S(1)}, f32[64,512]{1,0:T(8,128)}, u32[]{:S(2)}) copy-start(f32[64,512]{1,0:T(8,128)} %get-tuple-element.24) | copy-start | bytes 393220
  94.0 5.6 %copy-start.15 = (bf16[64,4,128]{2,1,0:T(4,128)(2,1)}, bf16[64,4,128]{2,1,0:T(4,128)(2,1)S(1)}, u32[]{:S(2)}) copy-start(bf16[64,4,128]{2,1,0:T(4,128)(2,1)S(1)} %multiply_convert_fusion.3) | copy-start | bytes 196612
  96.6 2.9 %copy-start.13 = (pred[64,2048]{1,0:T(8,128)(4,1)}, pred[64,2048]{1,0:T(8,128)(4,1)S(1)}, u32[]{:S(2)}) copy-start(pred[64,2048]{1,0:T(8,128)(4,1)S(1)} %iota_compare_fusion.1) | copy-start | bytes 393220
  131.1 4.9 %copy-start.10 = (f32[64,4,1,128]{3,1,0,2:T(4,128)S(1)}, f32[64,4,1,128]{3,1,0,2:T(4,128)}, u32[]{:S(2)}) copy-start(f32[64,4,1,128]{3,1,0,2:T(4,128)} %stack_reshape.13) | copy-start | bytes 393220
  131.2 4.7 %copy-start.7 = (bf16[64,512]{1,0:T(8,128)(2,1)}, bf16[64,512]{1,0:T(8,128)(2,1)S(1)}, u32[]{:S(2)}) copy-start(bf16[64,512]{1,0:T(8,128)(2,1)S(1)} %fusion.38) | copy-start | bytes 196612
  143.9 6.5 %copy-start.8 = (bf16[64,512]{1,0:T(8,128)(2,1)S(1)}, bf16[64,512]{1,0:T(8,128)(2,1)}, u32[]{:S(2)}) copy-start(bf16[64,512]{1,0:T(8,128)(2,1)} %copy-done.7) | copy-start | bytes 196612
  148.0 4.3 %copy-start.6 = (bf16[64,512]{1,0:T(8,128)(2,1)S(1)}, bf16[64,512]{1,0:T(8,128)(2,1)}, u32[]{:S(2)}) copy-start(bf16[64,512]{1,0:T(8,128)(2,1)} %get-tuple-element.42) | copy-start | bytes 196612
  149.3 13.8 %copy-start.1 = (bf16[512,1024]{1,0:T(8,128)(2,1)S(1)}, bf16[512,1024]{1,0:T(8,128)(2,1)}, u32[]{:S(2)}) copy-start(bf16[512,1024]{1,0:T(8,128)(2,1)} %param.13) | copy-start | bytes 3145732
  150.4 9.6 %copy-start.16 = (f32[128,1]{1,0:T(8,128)S(1)}, f32[128,1]{1,0:T(8,128)}, u32[]{:S(2)}) copy-start(f32[128,1]{1,0:T(8,128)} %get-tuple-element.23) | copy-start | bytes 1540
  150.4 9.7 %copy-start.3 = (f32[128,1024]{1,0:T(8,128)S(1)}, f32[128,1024]{1,0:T(8,128)}, u32[]{:S(2)}) copy-start(f32[128,1024]{1,0:T(8,128)} %get-tuple-element.29) | copy-start | bytes 1572868
  150.4 11.7 %copy-start.12 = (bf16[64,512]{1,0:T(8,128)(2,1)S(1)}, bf16[64,512]{1,0:T(8,128)(2,1)}, u32[]{:S(2)}) copy-start(bf16[64,512]{1,0:T(8,128)(2,1)} %copy-done.11) | copy-start | bytes 196612

commit v4 on v3

--- a/solution.py
+++ b/solution.py
@@ -505,10 +505,6 @@
     own_requests = candidate_row.shape[0]
     scaling = HEAD ** (-0.5)
 
-    sections = head_weights.reshape(width, heads, 4, HEAD)
-    gate_w, value_w, query_w, key_w = (
-        sections[:, :, index].reshape(width, cols) for index in range(4)
-    )
     (
         x_low,
         before_key,
@@ -582,48 +578,49 @@
         gated.astype(F32), own_picked, (((0,), (0,)), ((), ())), precision=HIGHEST
     )
 
-    slopes = jnp.einsum("qhd,khd->hqk", d_attended, values, preferred_element_type=F32)
-    d_logit = jnp.where(allowed, slopes * silu_slope(logits) / divisor, 0.0).astype(BF16)
-    d_query = jnp.einsum("hqk,khd->qhd", d_logit, key_heads, preferred_element_type=F32) * scaling
-    d_key = jnp.einsum("hqk,qhd->khd", d_logit, queries, preferred_element_type=F32) * scaling
-    d_value = jnp.einsum("hqk,qhd->khd", weight, d_attended, preferred_element_type=F32)
-
-    d_before_key = (d_key.reshape(length, cols) * silu_slope(before_key)).astype(BF16)
-    d_before_value = (d_value.reshape(length, cols) * silu_slope(before_value)).astype(BF16)
-    d_before_query = (d_query.reshape(requests, cols) * silu_slope(before_query)).astype(BF16)
-    d_before_gate = (d_gate * silu_slope(before_gate)).astype(BF16)
-
     def own_features(array):
         return lax.dynamic_slice_in_dim(array, ctx_index * merge_cols, merge_cols, 1)
 
-    def grad_of(rows, grads):
-        return split(lax.dot_general(rows, grads, (((0,), (0,)), ((), ())), preferred_element_type=F32))
-
-    x_own = own_features(x_low)
-    x_own_requests = own_features(x_requests)
-    grad_heads = jnp.stack(
-        [
-            grad_of(x_own_requests, d_before_gate),
-            grad_of(x_own, d_before_value),
-            grad_of(x_own_requests, d_before_query),
-            grad_of(x_own, d_before_key),
-        ],
-        2,
-    ).reshape(merge_cols, 4 * cols)
-
     def own_rows(array):
         return lax.dynamic_slice_in_dim(array, first_row, row_count, 0)
+
+    def over_rows(rows, grads):
+        return lax.dot_general(rows, grads, (((0,), (0,)), ((), ())), preferred_element_type=F32)
 
     positions = first_row + jnp.arange(row_count, dtype=jnp.int32)
     places = positions[:, None] == request_points[None, :]
     low_places = places.astype(BF16)
-    d_normed = core_sum(
-        back(own_rows(d_before_key), key_w)
-        + back(own_rows(d_before_value), value_w)
-        + back(mm(low_places, d_before_query).astype(BF16), query_w)
-        + back(mm(low_places, d_before_gate).astype(BF16), gate_w),
-        2,
-    )
+    x_own = own_features(x_low)
+    x_own_requests = own_features(x_requests)
+    head_grads = []
+    own_grads = []
+    for head in range(heads):
+        span = slice(head * HEAD, (head + 1) * HEAD)
+        slopes = back(d_attended[:, head], values[:, head])
+        d_logit = jnp.where(
+            allowed[0], slopes * silu_slope(logits[head]) / divisor[0], 0.0
+        ).astype(BF16)
+        d_query = mm(d_logit, key_heads[:, head]) * scaling
+        d_key = over_rows(d_logit, queries[:, head]) * scaling
+        d_value = over_rows(weight[head], d_attended[:, head])
+        key_grad = (d_key * silu_slope(before_key[:, span])).astype(BF16)
+        value_grad = (d_value * silu_slope(before_value[:, span])).astype(BF16)
+        query_grad = (d_query * silu_slope(before_query[:, span])).astype(BF16)
+        gate_grad = (d_gate[:, span] * silu_slope(before_gate[:, span])).astype(BF16)
+        head_grads += [
+            over_rows(x_own_requests, gate_grad),
+            over_rows(x_own, value_grad),
+            over_rows(x_own_requests, query_grad),
+            over_rows(x_own, key_grad),
+        ]
+        own_grads += [
+            mm(low_places, gate_grad).astype(BF16),
+            own_rows(value_grad),
+            mm(low_places, query_grad).astype(BF16),
+            own_rows(key_grad),
+        ]
+    grad_heads = jnp.concatenate(head_grads, 1)
+    d_normed = core_sum(back(jnp.concatenate(own_grads, 1), head_weights), 2)
     column_start = cand_index * slice_width
     d_input = lax.dynamic_slice_in_dim(
         norm_back(d_normed, x_normed, x_inverse), column_start, slice_width, 1

time: 164 us -> 177 us (1.079)
  matrix products: 35.3 us -> 48.2 us
  local copies, waits for them, and re-layouts: 28.1 us -> 22.2 us
  other arithmetic: 21.9 us -> 27 us
    reshape x3 -> x0, local copies, waits for them, and re-layouts: 11.7 us -> none  [the longest x1 5.37 us: per_device(): d_key.reshape(length, cols) * silu_slope(before_key)]
    dot_general x2 -> x14, matrix products: 1.73 us -> 9.89 us  [mm(): return jnp.dot(left, right, preferred_element_type=F32)]
    convert_element_type x2 -> x1, other arithmetic: 8.4 us -> 1.48 us  [per_device(): (d_gate[:, span] * silu_slope(before_gate[:, span])).astype(BF16)]
    dot_general x8 -> x24, matrix products: 18.4 us -> 24.5 us  [over_rows(): lax.dot_general(rows, grads, (((0,), (0,)), ((), ())), preferred_element_...]
    reshape x1 -> x3, local copies, waits for them, and re-layouts: 0.96 us -> 5.2 us  [split(): return array.reshape(array.shape[0], heads, HEAD)]
    unnamed x43 -> x85, local copies, waits for them, and re-layouts: 6.51 us -> 9 us
    another operation x5 -> x0, local copies, waits for them, and re-layouts: 2.08 us -> none  [per_device(): jnp.stack([grad_of(x_own_requests, d_before_gate), grad_of(x_own, d_befor...]
    dot_general x4 -> x5, matrix products: 6.76 us -> 4.89 us  [back(): lax.dot_general(grads, weights, (((1,), (1,)), ((), ())), preferred_eleme...]
where the time goes in v4:
time: 177 us; the launch traced here: 176 us
  Pallas kernels  70.8 us (40%)
  matrix products  48.2 us (27%)
  other arithmetic  27 us (15%)
  local copies, waits for them, and re-layouts  22.2 us (13%)
  blocking collectives  6.02 us (3%)
    pallas_call x1, Pallas kernels, gather_history(): pl.pallas_call(functools.partial(history_kernel, ctx_count, cand_count, h...  56.8 us
    dot_general x24, matrix products, over_rows(): lax.dot_general(rows, grads, (((0,), (0,)), ((), ())), preferred_element_...  24.5 us
    pallas_call x1, Pallas kernels, gather_user_grad(): pl.pallas_call(functools.partial(user_grad_kernel, ctx_count, cand_count)...  10.2 us
    dot_general x14, matrix products, mm(): return jnp.dot(left, right, preferred_element_type=F32)  9.89 us
    unnamed x85, local copies, waits for them, and re-layouts  9 us
    reshape x3, local copies, waits for them, and re-layouts, split(): return array.reshape(array.shape[0], heads, HEAD)  5.2 us
    dot_general x5, matrix products, back(): lax.dot_general(grads, weights, (((1,), (1,)), ((), ())), preferred_eleme...  4.89 us
    pallas_call x1, Pallas kernels, core_sum(): pl.pallas_call(functools.partial(core_sum_kernel, cand_count), out_shape=...  3.81 us

profile of v4, /device:TPU:0, one launch (start us, length us, event | category | flops | bytes accessed | tf_op | source)
XLA Modules:
  0.0 175.5 jit_solution(8237220948105988114)
XLA Ops:
  1.2 1.2 add_convert_fusion.2
  4.9 1.4 copy.176.points
  6.3 1.4 iota_compare_fusion.1
  7.7 56.8 %history_project.1 = (bf16[2048,1024]{1,0:T(8,128)(2,1)}, f32[2048,512]{1,0:T(8,128)}, f32[2048,512]{1,0:T(8,128)}, bf16[2048,512]{1,0:T(8,128)(2,1)}, bf16[2048...) custom-call(bf16[128,512]{1,0:T(8,128)(2,1)} %history.1, ...), custom_call_target="tpu_custom_call" | custom-call | tf_op jit(solution)/shard_map/history_project/pallas_call | solution.py:338
  64.6 1.5 reduce
  66.0 1.6 copy_bitcast_fusion.9
  67.6 1.0 reshape.103
  68.8 1.2 multiply_reduce_fusion.1
  71.1 1.1 fusion.61
  72.4 3.5 %psum.14 = f32[4,1024]{1,0:T(4,128)S(1)} all-reduce(f32[4,1024]{1,0:T(4,128)S(1)} %fusion.106), channel_id=1, replica_groups=mesh['ctx'=16,'cand'=2] {'cand'}, use_global_device_ids=true, to_apply=%region_2.3 | all-reduce | flops 4096 | bytes 32768 | tf_op jit(solution)/shard_map/psum | solution.py:546
  75.9 1.5 fusion.105
  77.4 2.7 %fusion.4 = f32[4,512]{1,0:T(4,128)S(1)} fusion(f32[512]{0:T(512)S(1)} %copy-done.31, f32[512,512]{1,0:T(8,128)} %get-tuple-element.22, f32[4,512]{1,0:T(4,128)S(1)} %fusion.105), kind=kLoop, calls=%fused_computation.7 | loop fusion | flops 7337984 | bytes 1067008 | tf_op jit(solution)/shard_map/reduce_sum | solution.py:554
  80.1 1.4 select_reduce_fusion.1
  81.5 2.5 %psum.15 = f32[4,512]{1,0:T(4,128)S(1)} all-reduce(f32[4,512]{1,0:T(4,128)S(1)} %select_reduce_fusion.1), channel_id=1, replica_groups=mesh['ctx'=16,'cand'=2] {'cand'}, use_global_device_ids=true, to_apply=%region_5.6 | all-reduce | flops 2048 | bytes 16384 | tf_op jit(solution)/shard_map/psum | solution.py:555
  84.8 1.2 select_reduce_fusion
  86.0 2.8 %fusion.8 = f32[4,512]{1,0:T(4,128)S(1)} fusion(f32[4,512]{1,0:T(4,128)S(1)} %select_reduce_fusion, f32[512,512]{1,0:T(8,128)} %get-tuple-element.22, f32[4,512]{1,0:T(4,128)S(1)} %fusion.105), kind=kLoop, calls=%fused_computation.11 | loop fusion | flops 10483712 | bytes 1073152 | tf_op jit(solution)/shard_map/reduce_sum | solution.py:562
  89.3 10.2 %user_grad_gather.1 = f32[16,4,512]{2,1,0:T(4,128)} custom-call(f32[4,512]{1,0:T(4,128)} %broadcast_multiply_fusion.part), custom_call_target="tpu_custom_call" | custom-call | tf_op jit(solution)/shard_map/user_grad_gather/pallas_call | solution.py:438
  99.5 1.0 reshape.104
  100.8 1.1 fusion.124
  101.9 2.2 %convert_multiply_fusion = (f32[64,512]{1,0:T(8,128)S(1)}, f32[64,512]{1,0:T(8,128)S(1)}) fusion(f32[64,512]{1,0:T(8,128)} %get-tuple-element.20, f32[8,8,4,128]{3,2,1,0:T(4,128)} %bitcast.194, f32[64,512]{1,0:T(8,128)S(1)} %copy-done.2, f32[8,8,4,128]{3,2,1,0:T(4,128)S(1)} %bitcast.192, f32[64,1024]{1,0:T(8,128)S(1)} %fusion.124, ...), kind=kOutput, calls=%fused_computation.131 | convolution fusion | flops 402980864 | bytes 2097152 | tf_op jit(solution)/shard_map/dot_general | solution.py:571
  104.1 1.5 fusion.76
  105.6 1.5 fusion.65
  107.0 1.0 fusion.80
  108.8 1.5 copy.184
  111.9 1.6 convolution_dynamic-update-slice_fusion.15
  113.5 1.5 fusion.41
  115.1 1.7 copy_bitcast_fusion
  116.8 2.5 %select_convert_fusion = (bf16[4,64,2048]{2,1,0:T(8,128)(2,1)S(1)}, f32[4,64,2048]{2,1,0:T(8,128)}) fusion(f32[64]{0:T(128)S(1)} %copy-done.35, pred[64,2048]{1,0:T(8,128)(4,1)S(1)} %copy-done.17, bf16[2048,512]{1,0:T(8,128)(2,1)S(1)} %copy-done.5, f32[64,512]{1,0:T(8,128)S(1)} %copy-done.16), kind=kOutput, calls=%fused_computation.54 | convolution fusion | flops 138575872 | bytes 5505280 | tf_op jit(solution)/shard_map/qhd,khd->hqk/dot_general | solution.py:536
  119.3 1.4 fusion.20
  120.7 1.4 fusion.18
  122.1 1.3 fusion.16
  124.0 2.2 %convolution_dynamic-update-slice_fusion.14 = f32[64,2048]{1,0:T(8,128)} fusion(f32[64,2048]{1,0:T(8,128)} %convolution_dynamic-update-slice_fusion.15, bf16[2048,128]{1,0:T(8,128)(2,1)S(1)} %fusion.14, bf16[2048,1024]{1,0:T(8,128)(2,1)} %get-tuple-element.31, s32[]{:T(128)S(6)} %select_n.58), kind=kOutput, calls=%fused_computation.70 | convolution fusion | flops 33554432 | bytes 1081348 | tf_op jit(solution)/shard_map/dot_general | solution.py:588
  126.7 2.5 %reshape.107 = bf16[2048,4,128]{2,1,0:T(4,128)(2,1)S(1)} reshape(bf16[2048,512]{1,0:T(8,128)(2,1)} %get-tuple-element.27) | data formatting | bytes 4194304 | tf_op jit(solution)/shard_map/reshape | solution.py:529
  129.3 3.3 %fusion.122 = (bf16[2048,1,128]{2,1,0:T(2,128)(2,1)S(1)}, bf16[2048,1,128]{2,1,0:T(2,128)(2,1)S(1)}, bf16[2048,1,128]{2,1,0:T(2,128)(2,1)S(1)}, bf16[2048,1,128]{2,1,0:T(2,128)(2,1)S(1)}) fusion(bf16[2048,4,128]{2,1,0:T(4,128)(2,1)S(1)} %reshape.107), kind=kLoop, calls=%fused_computation.244 | loop fusion | bytes 4194304 | tf_op jit(solution)/shard_map/slice | solution.py:599
  133.1 1.1 copy-done.6
  134.4 1.0 copy-done.33
  141.3 1.6 copy-done.4
  142.9 1.1 convolution_dynamic-update-slice_fusion.12
  146.4 1.1 convolution_dynamic-update-slice_fusion.10
  149.8 1.1 convolution_dynamic-update-slice_fusion.8
  153.2 1.1 convolution_dynamic-update-slice_fusion.6
  156.6 1.1 convolution_dynamic-update-slice_fusion.4
  160.0 1.1 convolution_dynamic-update-slice_fusion.2
  162.6 1.1 convolution_dynamic-update-slice_fusion
  165.1 3.4 %fusion.125.part = f32[128,1024]{1,0:T(8,128)} fusion(bf16[128,2048]{1,0:T(8,128)(2,1)} %constant_dynamic-update-slice_fusion, bf16[1024,2048]{1,0:T(8,128)(2,1)S(1)} %copy-done.1), kind=kOutput, calls=%fused_computation.247 | convolution fusion | flops 536870912 | bytes 5242880 | tf_op jit(solution)/shard_map/dot_general | solution.py:41
  168.5 3.8 %core_sum.1 = f32[128,1024]{1,0:T(8,128)} custom-call(f32[128,1024]{1,0:T(8,128)} %fusion.125.part), custom_call_target="tpu_custom_call" | custom-call | tf_op jit(solution)/shard_map/core_sum/pallas_call | solution.py:468
  172.3 1.2 fusion.121
  173.5 2.0 %convolution_add_fusion = f32[128,512]{1,0:T(8,128)} fusion(f32[128,1024]{1,0:T(8,128)S(1)} %copy-done.10, s32[]{:T(128)S(6)} %select_n.51, f32[128,1024]{1,0:T(8,128)} %core_sum.1, f32[128]{0:T(128)S(1)} %copy-done.30, f32[128]{0:T(128)S(1)} %broadcast_multiply_fusion.4, f32[128]{0:T(128)S(1)} %broadcast_multiply_fusion.5, f32[64,1024]{1,0:T(8,128)S(1)} %copy-done.8, ...), kind=kOutput, calls=%fused_computation.55 | convolution fusion | flops 50667520 | bytes 921088 | tf_op jit(solution)/shard_map/dot_general | solution.py:629
  (133 shorter events, 30.6 us)
Async XLA Ops:
  0.6 71.5 %copy-start = (bf16[512,1024]{1,0:T(8,128)(2,1)S(1)}, bf16[512,1024]{1,0:T(8,128)(2,1)}, u32[]{:S(2)}) copy-start(bf16[512,1024]{1,0:T(8,128)(2,1)} %param.13) | copy-start | bytes 3145732
  7.7 69.7 %copy-start.31 = (f32[512]{0:T(512)S(1)}, f32[512]{0:T(512)}, u32[]{:S(2)}) copy-start(f32[512]{0:T(512)} %param.17) | copy-start | bytes 6148
  64.5 15.6 %copy-start.27 = (s32[4,512]{1,0:T(4,128)S(1)}, s32[4,512]{1,0:T(4,128)}, u32[]{:S(2)}) copy-start(s32[4,512]{1,0:T(4,128)} %param.20) | copy-start | bytes 24580
  64.6 19.4 %copy-start.19 = (s32[4,512]{1,0:T(4,128)S(1)}, s32[4,512]{1,0:T(4,128)}, u32[]{:S(2)}) copy-start(s32[4,512]{1,0:T(4,128)} %param.21) | copy-start | bytes 24580
  67.6 32.9 %copy-start.28 = (s32[64]{0:T(128)S(1)}, s32[64]{0:T(128)}, u32[]{:S(2)}) copy-start(s32[64]{0:T(128)} %param.18) | copy-start | bytes 772
  68.6 32.2 %copy-start.3 = (bf16[1024,512]{1,0:T(8,128)(2,1)S(1)}, bf16[1024,512]{1,0:T(8,128)(2,1)}, u32[]{:S(2)}) copy-start(bf16[1024,512]{1,0:T(8,128)(2,1)} %get-tuple-element.21) | copy-start | bytes 3145732
  68.8 2.2 %copy-start.25 = (f32[64,4]{0,1:T(4,128)}, f32[64,4]{0,1:T(4,128)S(1)}, u32[]{:S(2)}) copy-start(f32[64,4]{0,1:T(4,128)S(1)} %broadcast_multiply_fusion.3) | copy-start | bytes 3076
  70.0 0.6 copy-start.26
  71.0 29.7 %copy-start.9 = (f32[64,4,128]{2,1,0:T(4,128)}, f32[64,4,128]{2,1,0:T(4,128)S(1)}, u32[]{:S(2)}) copy-start(f32[64,4,128]{2,1,0:T(4,128)S(1)} %mul.344.clone) | copy-start | bytes 393220
  72.1 17.2 %copy-start.14 = (bf16[64,512]{1,0:T(8,128)(2,1)}, bf16[64,512]{1,0:T(8,128)(2,1)S(1)}, u32[]{:S(2)}) copy-start(bf16[64,512]{1,0:T(8,128)(2,1)S(1)} %fusion.61) | copy-start | bytes 196612
  72.2 29.7 %copy-start.2 = (f32[64,512]{1,0:T(8,128)S(1)}, f32[64,512]{1,0:T(8,128)}, u32[]{:S(2)}) copy-start(f32[64,512]{1,0:T(8,128)} %get-tuple-element.19) | copy-start | bytes 393220
  100.5 6.5 %copy-start.15 = (bf16[64,512]{1,0:T(8,128)(2,1)S(1)}, bf16[64,512]{1,0:T(8,128)(2,1)}, u32[]{:S(2)}) copy-start(bf16[64,512]{1,0:T(8,128)(2,1)} %copy-done.14) | copy-start | bytes 196612
  101.9 5.2 %copy-start.7 = (f32[64,1024]{1,0:T(8,128)}, f32[64,1024]{1,0:T(8,128)S(1)}, u32[]{:S(2)}) copy-start(f32[64,1024]{1,0:T(8,128)S(1)} %fusion.124) | copy-start | bytes 786436
  101.9 13.2 %copy-start.5 = (bf16[2048,512]{1,0:T(8,128)(2,1)S(1)}, bf16[2048,512]{1,0:T(8,128)(2,1)}, u32[]{:S(2)}) copy-start(bf16[2048,512]{1,0:T(8,128)(2,1)} %get-tuple-element.25) | copy-start | bytes 6291460
  108.8 8.0 %copy-start.16 = (f32[64,512]{1,0:T(8,128)S(1)}, f32[64,512]{1,0:T(8,128)}, u32[]{:S(2)}) copy-start(f32[64,512]{1,0:T(8,128)} %get-tuple-element.24) | copy-start | bytes 393220
  110.3 6.5 %copy-start.17 = (pred[64,2048]{1,0:T(8,128)(4,1)S(1)}, pred[64,2048]{1,0:T(8,128)(4,1)}, u32[]{:S(2)}) copy-start(pred[64,2048]{1,0:T(8,128)(4,1)} %iota_compare_fusion.1) | copy-start | bytes 393220
  110.3 6.5 %copy-start.35 = (f32[64]{0:T(128)S(1)}, f32[64]{0:T(128)}, u32[]{:S(2)}) copy-start(f32[64]{0:T(128)} %add_convert_fusion.2) | copy-start | bytes 772
  111.9 11.5 %copy-start.23 = (bf16[64,4,128]{2,0,1:T(8,128)(2,1)}, bf16[64,4,128]{2,0,1:T(8,128)(2,1)S(1)}, u32[]{:S(2)}) copy-start(bf16[64,4,128]{2,0,1:T(8,128)(2,1)S(1)} %fusion.64) | copy-start | bytes 196612
  116.8 2.5 %copy-start.34 = (f32[2048,512]{1,0:T(8,128)S(1)}, f32[2048,512]{1,0:T(8,128)}, u32[]{:S(2)}) copy-start(f32[2048,512]{1,0:T(8,128)} %get-tuple-element.26) | copy-start | bytes 12582916
  129.3 3.4 %copy-start.24 = (bf16[64,4,128]{2,0,1:T(8,128)(2,1)S(1)}, bf16[64,4,128]{2,0,1:T(8,128)(2,1)}, u32[]{:S(2)}) copy-start(bf16[64,4,128]{2,0,1:T(8,128)(2,1)} %copy-done.23) | copy-start | bytes 196612
  129.3 3.4 %copy-start.29 = (s32[64]{0:T(128)S(1)}, s32[64]{0:T(128)}, u32[]{:S(2)}) copy-start(s32[64]{0:T(128)} %param.18) | copy-start | bytes 772
  129.3 3.4 %copy-start.36 = (f32[64]{0:T(128)S(1)}, f32[64]{0:T(128)}, u32[]{:S(2)}) copy-start(f32[64]{0:T(128)} %add_convert_fusion.2) | copy-start | bytes 772
  129.3 3.4 %copy-start.37 = (f32[4,64,2048]{2,1,0:T(8,128)S(1)}, f32[4,64,2048]{2,1,0:T(8,128)}, u32[]{:S(2)}) copy-start(f32[4,64,2048]{2,1,0:T(8,128)} %get-tuple-element.49) | copy-start | bytes 6291460
  132.6 1.6 copy-start.6
  132.6 1.8 %copy-start.20 = (bf16[64,4,128]{2,0,1:T(8,128)(2,1)S(1)}, bf16[64,4,128]{2,0,1:T(8,128)(2,1)}, u32[]{:S(2)}) copy-start(bf16[64,4,128]{2,0,1:T(8,128)(2,1)} %copy_bitcast_fusion.9) | copy-start | bytes 196612
  132.6 2.8 %copy-start.33 = (f32[2048,512]{1,0:T(8,128)S(1)}, f32[2048,512]{1,0:T(8,128)}, u32[]{:S(2)}) copy-start(f32[2048,512]{1,0:T(8,128)} %get-tuple-element.28) | copy-start | bytes 12582916
  137.6 0.9 copy-start.18
  137.6 1.8 %copy-start.32 = (s32[128]{0:T(128)S(1)}, s32[128]{0:T(128)}, u32[]{:S(2)}) copy-start(s32[128]{0:T(128)} %iota_add_fusion) | copy-start | bytes 1540
  140.7 2.2 %copy-start.4 = (bf16[2048,1024]{1,0:T(8,128)(2,1)S(1)}, bf16[2048,1024]{1,0:T(8,128)(2,1)}, u32[]{:S(2)}) copy-start(bf16[2048,1024]{1,0:T(8,128)(2,1)} %get-tuple-element.31) | copy-start | bytes 12582916
  140.7 3.9 %copy-start.22 = (bf16[64,128]{1,0:T(8,128)(2,1)S(1)}, bf16[64,128]{1,0:T(8,128)(2,1)}, u32[]{:S(2)}) copy-start(bf16[64,128]{1,0:T(8,128)(2,1)} %get-tuple-element.42) | copy-start | bytes 49156
  140.8 5.6 %copy-start.13 = (bf16[2048,128]{1,0:T(8,128)(2,1)S(1)}, bf16[2048,128]{1,0:T(8,128)(2,1)}, u32[]{:S(2)}) copy-start(bf16[2048,128]{1,0:T(8,128)(2,1)} %fusion.16) | copy-start | bytes 1572868
  140.8 10.7 %copy-start.21 = (bf16[64,128]{1,0:T(8,128)(2,1)S(1)}, bf16[64,128]{1,0:T(8,128)(2,1)}, u32[]{:S(2)}) copy-start(bf16[64,128]{1,0:T(8,128)(2,1)} %get-tuple-element.41) | copy-start | bytes 49156
  140.8 12.4 %copy-start.12 = (bf16[2048,128]{1,0:T(8,128)(2,1)S(1)}, bf16[2048,128]{1,0:T(8,128)(2,1)}, u32[]{:S(2)}) copy-start(bf16[2048,128]{1,0:T(8,128)(2,1)} %fusion.18) | copy-start | bytes 1572868
  142.9 17.1 %copy-start.11 = (bf16[2048,128]{1,0:T(8,128)(2,1)S(1)}, bf16[2048,128]{1,0:T(8,128)(2,1)}, u32[]{:S(2)}) copy-start(bf16[2048,128]{1,0:T(8,128)(2,1)} %fusion.20) | copy-start | bytes 1572868
  142.9 22.2 %copy-start.1 = (bf16[1024,2048]{1,0:T(8,128)(2,1)S(1)}, bf16[1024,2048]{1,0:T(8,128)(2,1)}, u32[]{:S(2)}) copy-start(bf16[1024,2048]{1,0:T(8,128)(2,1)} %head_weights.1) | copy-start | bytes 12582916
  160.0 12.3 %copy-start.10 = (f32[128,1024]{1,0:T(8,128)S(1)}, f32[128,1024]{1,0:T(8,128)}, u32[]{:S(2)}) copy-start(f32[128,1024]{1,0:T(8,128)} %get-tuple-element.29) | copy-start | bytes 1572868
  162.6 10.9 %copy-start.8 = (f32[64,1024]{1,0:T(8,128)S(1)}, f32[64,1024]{1,0:T(8,128)}, u32[]{:S(2)}) copy-start(f32[64,1024]{1,0:T(8,128)} %copy-done.7) | copy-start | bytes 786436
  162.6 11.0 %copy-start.30 = (f32[128]{0:T(128)S(1)}, f32[128]{0:T(128)}, u32[]{:S(2)}) copy-start(f32[128]{0:T(128)} %reduce) | copy-start | bytes 1540
